TPU v7x, 32 devices: a whole 2x2x4 slice. The times are simulated.
32 devices in a mesh: blk: 8 (over y, x, core), rep: 4 (over z).
Axes of the slice: x: 2, y: 2, z: 4, core: 2. Of those that a mesh axis runs over, the one named last changes fastest.
Arguments:
- node_states: float32 [4096, 128], P('blk'), may hold values from -6 to 6
- edge_feats: bfloat16 [32768, 16], P('blk'), may hold values from -6 to 6
- edge_source: int32 [32768], P('blk'), may hold values from 0 to 4095, as said below
- edge_target: int32 [32768], P('blk'), may hold values from 0 to 4095, as said below
- edge_group: int32 [32768], P('blk'), may hold values from 0 to 15
- column_mask: int32 [16, 16], replicated, may hold values 0 or 1
- edge_count: int32 [8], P('blk'), may hold values from 2048 to 4096, as said below
- first_weight: bfloat16 [16, 128], replicated, may hold values from -1.5 to 1.5
- first_bias: float32 [128], replicated, may hold values from -3 to 3
- second_weight: bfloat16 [128, 16384], P(None, 'rep'), may hold values from -0.046875 to 0.046875
- second_bias: float32 [16384], P('rep'), may hold values from -0.3125 to 0.3125
- update_input_weight: bfloat16 [128, 384], replicated, may hold values from -0.5 to 0.5
- update_state_weight: bfloat16 [128, 384], replicated, may hold values from -0.5 to 0.5
- update_input_bias: float32 [384], replicated, may hold values from -1.75 to 1.75
- update_state_bias: float32 [384], replicated, may hold values from -1.75 to 1.75
- state_cotangent: float32 [4096, 128], P('blk'), may hold values from -6 to 6
Outputs:
- final_states: float32 [4096, 128], P('blk')
- grad_states: float32 [4096, 128], P('blk')
- grad_edge_feats: float32 [32768, 16], P('blk')
- grad_first_weight: float32 [16, 128], replicated
- grad_first_bias: float32 [128], replicated
- grad_second_weight: float32 [128, 16384], P(None, 'rep')
- grad_second_bias: float32 [16384], P('rep')
- grad_input_weight: float32 [128, 384], replicated
- grad_state_weight: float32 [128, 384], replicated
- grad_input_bias: float32 [384], replicated
- grad_state_bias: float32 [384], replicated
Inputs may be any that keep to these rules, and one draw needn't show every extreme that they name: `edge_source`: the graph is split into node blocks of 512 nodes. Of the 4096 edge slots of block b, exactly 256 have a source in each other block and the remaining 2304 a source in block b itself, in no particular order. `edge_target`: edges held by index b of blk point to nodes b * 512 to (b + 1) * 512 - 1 of that block, in non-decreasing order. The first edge_count[b] slots of block b are live edges, the others are padding. One block is full and one holds half of 4096.
All inputs are finite; a program needn't handle non-finite values.
Results may differ from a plain program's by a relative error of at most 0.008.
The roundings to bfloat16 on the way count: a program that leaves them out, or rounds other values in their place, can miss the bound.
Values may be sent and summed in bfloat16 or wider, within the bound.
A program may use at most 128 MiB of HBM per device.

v0:
```python
import jax
import jax.numpy as jnp
from jax import lax
from jax.sharding import PartitionSpec as P

STEPS = 2


def pull_rows(gathered, shard_piece, edge_source):
    inside = (edge_source >= 0) & (edge_source < shard_piece.shape[0])
    taken_rows = jnp.take(shard_piece, jnp.clip(edge_source, 0, shard_piece.shape[0] - 1), axis=0)
    return jnp.where(inside[:, None], taken_rows, gathered)


def body(
    node_states,
    edge_feats,
    edge_source,
    edge_target,
    edge_group,
    column_mask,
    edge_count,
    first_weight,
    first_bias,
    second_weight,
    second_bias,
    update_input_weight,
    update_state_weight,
    update_input_bias,
    update_state_bias,
    state_cotangent,
):
    highest = lax.Precision.HIGHEST
    f32 = jnp.float32
    bf16 = jnp.bfloat16
    node_rows = node_states.shape[0]
    width = node_states.shape[1]
    edge_rows = edge_source.shape[0]
    rep_size = lax.axis_size("rep")
    part_rows = width // rep_size
    column_start = lax.axis_index("rep") * part_rows
    target_local = edge_target - lax.axis_index("blk") * node_rows
    live_edge = (jnp.arange(edge_rows, dtype=jnp.int32) < edge_count[0]).astype(f32)
    group_onehot = (
        edge_group[:, None] == jnp.arange(column_mask.shape[0], dtype=jnp.int32)[None, :]
    ).astype(bf16)
    group_mask = jnp.dot(group_onehot, column_mask.astype(bf16), preferred_element_type=f32)
    masked = (edge_feats.astype(f32) * group_mask).astype(bf16)
    block_rows = min(256, edge_rows)
    block_total = edge_rows // block_rows
    feat_blocks = masked.reshape(block_total, block_rows, masked.shape[1])
    live_blocks = live_edge.reshape(block_total, block_rows)

    def edge_matrices(feat_block):
        pre = jnp.dot(feat_block, first_weight, preferred_element_type=f32) + first_bias
        hidden_low = jax.nn.silu(pre).astype(bf16)
        flat = jnp.dot(hidden_low, second_weight, preferred_element_type=f32) + second_bias
        return (hidden_low, flat.astype(bf16).reshape(feat_block.shape[0], part_rows, width))

    def gate_values(summed_low, state_low):
        input_gates = (
            jnp.dot(summed_low, update_input_weight, preferred_element_type=f32) + update_input_bias
        )
        state_gates = (
            jnp.dot(state_low, update_state_weight, preferred_element_type=f32) + update_state_bias
        )
        reset = jax.nn.sigmoid(input_gates[:, :width] + state_gates[:, :width])
        update = jax.nn.sigmoid(
            input_gates[:, width : 2 * width] + state_gates[:, width : 2 * width]
        )
        state_part = state_gates[:, 2 * width :]
        candidate = jnp.tanh(input_gates[:, 2 * width :] + reset * state_part)
        return (reset, update, candidate, state_part)

    def message_block(unused, pieces):
        feat_block, source_block_rows, live_block = pieces
        hidden_low, matrices = edge_matrices(feat_block)
        message = jnp.einsum("eij,ej->ei", matrices, source_block_rows, preferred_element_type=f32)
        return (unused, message * live_block[:, None])

    state = node_states
    history = []
    for layer_step in range(STEPS):
        state_low = state.astype(bf16)
        empty_sources = jnp.zeros((edge_rows, width), bf16)
        sources = pull_rows(
            empty_sources, lax.all_gather(state_low, "blk", axis=0, tiled=True), edge_source
        )
        unused, messages = lax.scan(
            message_block,
            0,
            (feat_blocks, sources.reshape(block_total, block_rows, width), live_blocks),
        )
        summed = jax.ops.segment_sum(
            messages.reshape(edge_rows, part_rows), target_local, num_segments=node_rows
        )
        summed_low = lax.all_gather(summed.astype(bf16), "rep", axis=1, tiled=True)
        reset, update, candidate, state_part = gate_values(summed_low, state_low)
        history.append((state, state_low, summed_low, sources))
        state = (1.0 - update) * candidate + update * state

    def grad_block(totals, pieces):
        feat_block, source_block_rows, dmsg_block = pieces
        hidden_low, matrices = edge_matrices(feat_block)
        outer = dmsg_block.astype(f32)[:, :, None] * source_block_rows.astype(f32)[:, None, :]
        outer_low = outer.reshape(feat_block.shape[0], part_rows * width).astype(bf16)
        grad_second = totals[0] + jnp.dot(hidden_low.T, outer_low, preferred_element_type=f32)
        grad_bias = totals[1] + jnp.sum(outer_low.astype(f32), axis=0)
        grad_hidden = jnp.dot(outer_low, second_weight.T, preferred_element_type=f32)
        grad_source = jnp.einsum("eij,ei->ej", matrices, dmsg_block, preferred_element_type=f32)
        return ((grad_second, grad_bias), (grad_hidden, grad_source))

    grad = state_cotangent
    grad_input_weight = jnp.zeros(update_input_weight.shape, f32)
    grad_state_weight = jnp.zeros(update_state_weight.shape, f32)
    grad_input_bias = jnp.zeros(update_input_bias.shape, f32)
    grad_state_bias = jnp.zeros(update_state_bias.shape, f32)
    second_totals = (jnp.zeros(second_weight.shape, f32), jnp.zeros(second_bias.shape, f32))
    hidden_grad = jnp.zeros((edge_rows, first_weight.shape[1]), f32)
    for layer_step in reversed(range(STEPS)):
        state_before, state_low, summed_low, sources = history[layer_step]
        reset, update, candidate, state_part = gate_values(summed_low, state_low)
        grad_cand = grad * (1.0 - update)
        grad_update = grad * (state_before - candidate)
        grad_pn = grad_cand * (1.0 - candidate * candidate)
        grad_pz = grad_update * update * (1.0 - update)
        grad_pr = grad_pn * state_part * reset * (1.0 - reset)
        input_delta = jnp.concatenate([grad_pr, grad_pz, grad_pn], axis=1)
        state_delta = jnp.concatenate([grad_pr, grad_pz, grad_pn * reset], axis=1)
        grad_input_weight = grad_input_weight + jnp.dot(
            summed_low.astype(f32).T, input_delta, precision=highest
        )
        grad_state_weight = grad_state_weight + jnp.dot(
            state_low.astype(f32).T, state_delta, precision=highest
        )
        grad_input_bias = grad_input_bias + jnp.sum(input_delta, axis=0)
        grad_state_bias = grad_state_bias + jnp.sum(state_delta, axis=0)
        summed_grad = jnp.dot(
            input_delta, update_input_weight.astype(f32).T, precision=highest
        ).astype(bf16)
        state_low_grad = jnp.dot(state_delta, update_state_weight.astype(f32).T, precision=highest)
        local_grad = lax.dynamic_slice_in_dim(summed_grad, column_start, part_rows, 1)
        message_grad = (
            jnp.take(local_grad, target_local, axis=0).astype(f32) * live_edge[:, None]
        ).astype(bf16)
        second_totals, (grad_hidden, grad_source) = lax.scan(
            grad_block,
            second_totals,
            (
                feat_blocks,
                sources.reshape(block_total, block_rows, width),
                message_grad.reshape(block_total, block_rows, part_rows),
            ),
        )
        hidden_grad = hidden_grad + grad_hidden.reshape(edge_rows, hidden_grad.shape[1])
        source_grad = grad_source.reshape(edge_rows, width)

        def spread(first_row, row_count, source_grad=source_grad):
            inside = (edge_source >= 0) & (edge_source < row_count)
            values = jnp.where(inside[:, None], source_grad, 0.0)
            return jax.ops.segment_sum(
                values, jnp.clip(edge_source, 0, row_count - 1), num_segments=row_count
            )

        partial_nodes = lax.psum_scatter(
            spread(jnp.int32(0), node_rows * lax.axis_size("blk")),
            "blk",
            scatter_dimension=0,
            tiled=True,
        )
        from_edges = lax.psum(partial_nodes, "rep")
        grad = grad * update + state_low_grad + from_edges
    pre = jnp.dot(masked, first_weight, preferred_element_type=f32) + first_bias
    sig_pre = jax.nn.sigmoid(pre)
    pre_grad = hidden_grad * sig_pre * (1.0 + pre * (1.0 - sig_pre))
    grad_first_weight = jnp.dot(masked.astype(f32).T, pre_grad, precision=highest)
    grad_first_bias = jnp.sum(pre_grad, axis=0)
    grad_edge_feats = jnp.dot(pre_grad, first_weight.astype(f32).T, precision=highest) * group_mask
    grad_edge_feats, grad_first_weight, grad_first_bias = lax.psum(
        (grad_edge_feats, grad_first_weight, grad_first_bias), "rep"
    )
    summed_weights = lax.psum(
        (
            grad_first_weight,
            grad_first_bias,
            second_totals[0],
            second_totals[1],
            grad_input_weight,
            grad_state_weight,
            grad_input_bias,
            grad_state_bias,
        ),
        "blk",
    )
    return (
        state,
        grad,
        grad_edge_feats,
        summed_weights[0],
        summed_weights[1],
        summed_weights[2],
        summed_weights[3],
        summed_weights[4],
        summed_weights[5],
        summed_weights[6],
        summed_weights[7],
    )


def solution(mesh):
    in_specs = (
        P("blk", None),
        P("blk", None),
        P("blk"),
        P("blk"),
        P("blk"),
        P(),
        P("blk"),
        P(),
        P(),
        P(None, "rep"),
        P("rep"),
        P(),
        P(),
        P(),
        P(),
        P("blk", None),
    )
    out_specs = (
        P("blk", None),
        P("blk", None),
        P("blk", None),
        P(),
        P(),
        P(None, "rep"),
        P("rep"),
        P(),
        P(),
        P(),
        P(),
    )
    return jax.shard_map(body, mesh=mesh, in_specs=in_specs, out_specs=out_specs, check_vma=False)
```

profile of v0, /device:TPU:0, one launch (start us, length us, event | category | flops | bytes accessed | tf_op | source)
XLA Modules:
  0.0 1115.8 jit_solution(2746004767982860255)
XLA Ops:
  18.9 17.8 %all-gather.3.cloned.1.call-done = bf16[4096,128]{1,0:T(8,128)(2,1)} async-done(((bf16[512,128]{1,0:T(8,128)(2,1)}), bf16[4096,128]{1,0:T(8,128)(2,1)}) %all-gather.3.cloned.1.call-update) | async-done | bytes 1048592 | tf_op jit(solution)/shard_map/all_gather | solution.py:87
  36.8 12.4 %gather_fusion = bf16[4096,128]{1,0:T(8,128)(2,1)S(1)} fusion(bf16[4096,128]{1,0:T(8,128)(2,1)} %all-gather.3.cloned.1.call-done, s32[4096]{0:T(1024)S(1)} %get-tuple-element.728), kind=kCustom, calls=%fused_computation.clone | custom fusion | bytes 2113536 | tf_op jit(solution)/shard_map/jit(_take)/gather | solution.py:11
  53.2 77.7 %while.53 = (s32[]{:T(128)}, f32[16,256,32]{2,1,0:T(8,128)}, bf16[16,256,16]{1,2,0:T(8,128)(2,1)}, bf16[16,128]{1,0:T(8,128)(2,1)S(1)}, f32[128]{0:T(128)S(1)}, ...) while((s32[]{:T(128)}, f32[16,256,32]{2,1,0:T(8,128)}, ...), condition=%wide.region_1.3_spmd, body=%wide.region_0.2_spmd.sunk | while | flops 273883136 | bytes 9862781 | solution.py:89
  131.0 26.8 %scatter_custom_fusion = f32[512,32]{1,0:T(8,128)S(1)} fusion(s32[4096]{0:T(1024)S(1)} %get-tuple-element.711, f32[4096,32]{1,0:T(8,128)} %bitcast.285, f32[]{:T(128)} %constant.102.clone.1), kind=kCustom, calls=%fused_computation.168 | custom fusion | flops 131072 | bytes 66048 | tf_op jit(solution)/shard_map/scatter-add | solution.py:94
  157.9 13.4 %all_gather.13 = bf16[512,128]{0,1:T(8,128)(2,1)S(1)} all-gather(bf16[512,32]{0,1:T(8,128)(2,1)S(1)} %copy.130), channel_id=1, replica_groups=mesh['blk'=8,'rep'=4] {'rep'}, dimensions={1}, use_global_device_ids=true | all-gather | bytes 163840 | tf_op jit(solution)/shard_map/all_gather | solution.py:97
  177.9 19.7 %all-gather.5.cloned.1.call-done = bf16[4096,128]{0,1:T(8,128)(2,1)} async-done(((bf16[512,128]{0,1:T(8,128)(2,1)}), bf16[4096,128]{0,1:T(8,128)(2,1)}) %all-gather.5.cloned.1.call-update) | async-done | bytes 1048592 | tf_op jit(solution)/shard_map/all_gather | solution.py:87
  199.9 15.6 %gather_fusion.1 = bf16[4096,128]{1,0:T(8,128)(2,1)} fusion(bf16[4096,128]{1,0:T(8,128)(2,1)} %copy.132, s32[4096]{0:T(1024)S(1)} %get-tuple-element.728), kind=kCustom, calls=%fused_computation.2.clone | custom fusion | bytes 2113536 | tf_op jit(solution)/shard_map/jit(_take)/gather | solution.py:11
  215.5 5.6 select_select_fusion
  222.6 124.8 %while.54 = (s32[]{:T(128)}, f32[16,256,32]{2,1,0:T(8,128)}, bf16[16,256,16]{1,2,0:T(8,128)(2,1)}, bf16[16,128]{1,0:T(8,128)(2,1)S(1)}, f32[128]{0:T(128)S(1)}, ...) while((s32[]{:T(128)}, f32[16,256,32]{2,1,0:T(8,128)}, ...), condition=%wide.region_4.6_spmd, body=%wide.region_3.5_spmd.sunk | while | flops 273883136 | bytes 9862781 | solution.py:89
  222.6 2.9 fusion.216
  230.4 2.9 fusion.216
  238.2 2.9 fusion.216
  246.0 2.9 fusion.216
  253.8 2.9 fusion.216
  261.6 2.9 fusion.216
  269.4 2.9 fusion.216
  277.2 2.9 fusion.216
  285.0 2.9 fusion.216
  292.8 2.9 fusion.216
  300.6 2.9 fusion.216
  308.4 2.9 fusion.216
  316.2 2.9 fusion.216
  324.0 2.9 fusion.216
  331.8 2.9 fusion.216
  339.6 2.9 fusion.216
  347.4 27.4 %scatter_custom_fusion.1 = f32[512,32]{1,0:T(8,128)} fusion(s32[4096]{0:T(1024)S(1)} %get-tuple-element.711, f32[4096,32]{1,0:T(8,128)} %bitcast.286, f32[]{:T(128)} %constant.102.clone.1), kind=kCustom, calls=%fused_computation.166 | custom fusion | flops 131072 | bytes 66048 | tf_op jit(solution)/shard_map/scatter-add | solution.py:94
  375.8 13.7 %all_gather.15 = bf16[512,128]{0,1:T(8,128)(2,1)S(1)} all-gather(bf16[512,32]{0,1:T(8,128)(2,1)S(1)} %copy.134), channel_id=1, replica_groups=mesh['blk'=8,'rep'=4] {'rep'}, dimensions={1}, use_global_device_ids=true | all-gather | bytes 163840 | tf_op jit(solution)/shard_map/all_gather | solution.py:97
  394.8 15.0 %gather_fusion.2 = bf16[4096,32]{1,0:T(8,128)(2,1)} fusion(bf16[512,32]{1,0:T(8,128)(2,1)S(1)} %copy.138, s32[4096]{0:T(1024)S(1)} %fusion.105), kind=kCustom, calls=%fused_computation.1.clone | custom fusion | bytes 540672 | tf_op jit(solution)/shard_map/jit(_take)/gather | solution.py:144
  409.8 4.0 multiply_convert_fusion.7
  416.9 204.7 %while.56 = (s32[]{:T(128)}, f32[128,4096]{1,0:T(8,128)S(1)}, f32[4096]{0:T(1024)S(1)}, f32[16,256,128]{2,1,0:T(8,128)}, f32[16,256,128]{2,1,0:T(8,128)}, /*inde...) while((s32[]{:T(128)}, f32[128,4096]{1,0:T(8,128)S(1)}, ...), condition=%wide.region_8.11_spmd.clone, body=%wide.region_6.10_spmd.clone.sunk | while | flops 816033792 | bytes 30618312 | solution.py:146
  419.6 3.1 convert_reduce_fusion.5
  432.4 3.1 convert_reduce_fusion.5
  445.1 3.1 convert_reduce_fusion.5
  457.9 3.1 convert_reduce_fusion.5
  470.7 3.1 convert_reduce_fusion.5
  483.5 3.1 convert_reduce_fusion.5
  496.3 3.1 convert_reduce_fusion.5
  499.4 2.9 convolution_add_fusion.21
  509.1 3.1 convert_reduce_fusion.5
  521.9 3.1 convert_reduce_fusion.5
  534.7 3.1 convert_reduce_fusion.5
  547.5 3.1 convert_reduce_fusion.5
  560.3 3.1 convert_reduce_fusion.5
  573.1 3.1 convert_reduce_fusion.5
  585.9 3.1 convert_reduce_fusion.5
  598.7 3.1 convert_reduce_fusion.5
  611.4 3.1 convert_reduce_fusion.5
  621.6 4.7 bitcast_select_fusion.1
  626.3 24.1 %scatter_custom_fusion.2 = f32[4096,128]{1,0:T(8,128)} fusion(s32[4096]{0:T(1024)} %get-tuple-element.727, f32[4096,128]{1,0:T(8,128)} %bitcast_select_fusion.1, f32[]{:T(128)} %constant.102.clone.1), kind=kCustom, calls=%fused_computation.113 | custom fusion | flops 524288 | bytes 2097664 | tf_op jit(solution)/shard_map/scatter-add | solution.py:161
  650.4 2.9 copy.140
  653.3 41.4 %reduce-scatter.3.cloned.1.call-done = f32[512,128]{0,1:T(8,128)} async-done(((f32[4096,128]{0,1:T(8,128)}), f32[512,128]{0,1:T(8,128)}) %reduce-scatter.3.cloned.1.call-update) | async-done | bytes 262160 | tf_op jit(solution)/shard_map/reduce_scatter | solution.py:165
  695.0 37.4 %all-reduce.8.cloned.1.call-done = f32[512,128]{0,1:T(8,128)} async-done(((f32[512,128]{0,1:T(8,128)}), f32[512,128]{0,1:T(8,128)}) %all-reduce.8.cloned.1.call-update) | async-done | bytes 262160 | tf_op jit(solution)/shard_map/psum | solution.py:171
  732.4 3.2 fusion.115
  737.7 14.9 %gather_fusion.3 = bf16[4096,32]{1,0:T(8,128)(2,1)} fusion(bf16[512,32]{1,0:T(8,128)(2,1)S(1)} %copy.143, s32[4096]{0:T(1024)S(1)} %fusion.105), kind=kCustom, calls=%fused_computation.3.clone | custom fusion | bytes 540672 | tf_op jit(solution)/shard_map/jit(_take)/gather | solution.py:144
  752.6 4.0 multiply_convert_fusion.6
  759.7 159.4 %while.55 = (s32[]{:T(128)}, f32[128,4096]{1,0:T(8,128)S(1)}, f32[4096]{0:T(1024)S(1)}, f32[16,256,128]{2,1,0:T(8,128)}, f32[16,256,128]{2,1,0:T(8,128)}, /*inde...) while((s32[]{:T(128)}, f32[128,4096]{1,0:T(8,128)S(1)}, ...), condition=%wide.region_14.17_spmd, body=%wide.region_12.16_spmd.sunk | while | flops 815505408 | bytes 22229656 | solution.py:146
  919.1 5.3 bitcast_select_fusion
  924.4 24.1 %scatter_custom_fusion.3 = f32[4096,128]{1,0:T(8,128)} fusion(s32[4096]{0:T(1024)} %get-tuple-element.727, f32[4096,128]{1,0:T(8,128)} %bitcast_select_fusion, f32[]{:T(128)} %constant.102.clone.1), kind=kCustom, calls=%fused_computation.111 | custom fusion | flops 524288 | bytes 2097664 | tf_op jit(solution)/shard_map/scatter-add | solution.py:161
  948.5 3.0 copy.145
  957.8 34.8 %reduce-scatter.5.cloned.1.call-done = f32[512,128]{0,1:T(8,128)} async-done(((f32[4096,128]{0,1:T(8,128)}), f32[512,128]{0,1:T(8,128)}) %reduce-scatter.5.cloned.1.call-update) | async-done | bytes 262160 | tf_op jit(solution)/shard_map/reduce_scatter | solution.py:165
  1002.1 12.5 %all-reduce.2 = (f32[16,128]{1,0:T(8,128)S(1)}, f32[128]{0:T(128)S(1)}) all-reduce(f32[16,128]{1,0:T(8,128)S(1)} %fusion.123, f32[128]{0:T(128)S(1)} %get-tuple-element.734), channel_id=1, replica_groups=mesh['blk'=8,'rep'=4] {'rep'}, use_global_device_ids=true, to_apply=%region_19.22 | all-reduce | flops 2176 | bytes 17408 | tf_op jit(solution)/shard_map/psum | solution.py:179
  1014.6 23.5 %all-reduce = (f32[16,128]{1,0:T(8,128)}, f32[128]{0:T(128)}, f32[4096]{0:T(1024)}, f32[384]{0:T(512)}, f32[384]{0:T(512)}) all-reduce(f32[16,128]{1,0:T(8,128)S(1)} %get-tuple-element.700, f32[128]{0:T(128)S(1)} %get-tuple-element.701, f32[4096]{0:T(1024)S(1)} %get-tuple-element.246, ...), channel_id=1, replica_groups=mesh['blk'=8,'rep'=4] {'blk'}, use_global_device_ids=true, to_apply=%region_20.23 | all-reduce | flops 7040 | bytes 56320 | tf_op jit(solution)/shard_map/psum | solution.py:182
  1040.4 62.9 %all-reduce.10.cloned.1.call-done = (f32[128,4096]{1,0:T(8,128)}, f32[128,384]{1,0:T(8,128)}, f32[128,384]{1,0:T(8,128)}) async-done(((f32[128,4096]{1,0:T(8,128)}, f32[128,384]{1,0:T(8,128)}, f32[128,384]{1,0:T(8,128)}), (f32[128,4096]{1,0:T(8,128)}, f32[128,384]{1,0:T(8,128)}, f32[128,384]{1,0:T(8,128)})) %all-reduce.10.cloned.1.call-update) | async-done | bytes 2490384 | tf_op jit(solution)/shard_map/psum | solution.py:182
  1104.0 3.2 copy.286
  (701 shorter events, 525.6 us)
Async XLA Ops:
  7.2 9.6 copy-start
  7.2 29.6 %all-gather.3.cloned.1.call-start = ((), (), s32[]{:S(2)}) async-start(), calls=%async_computation.2 | async-start | bytes 1179648 | tf_op jit(solution)/shard_map/all_gather | solution.py:87
  8.9 188.8 %all-gather.5.cloned.1.call-start = ((), (), s32[]{:S(2)}) async-start(), calls=%async_computation.3 | async-start | bytes 1179648 | tf_op jit(solution)/shard_map/all_gather | solution.py:87
  12.6 36.6 %copy-start.27 = (bf16[4096,16]{0,1:T(8,128)(2,1)}, bf16[4096,16]{0,1:T(8,128)(2,1)S(1)}, u32[]{:S(2)}) copy-start(bf16[4096,16]{0,1:T(8,128)(2,1)S(1)} %get-tuple-element.731) | copy-start | bytes 393220
  49.2 4.0 copy-start.1
  49.2 4.0 copy-start.7
  49.2 4.0 copy-start.35
  49.2 4.0 copy-start.42
  53.2 118.1 %copy-start.36 = (bf16[128,384]{1,0:T(8,128)(2,1)S(1)}, bf16[128,384]{1,0:T(8,128)(2,1)}, u32[]{:S(2)}) copy-start(bf16[128,384]{1,0:T(8,128)(2,1)} %param.39) | copy-start | bytes 294916
  53.2 118.1 %copy-start.44 = (f32[384]{0:T(512)S(1)}, f32[384]{0:T(512)}, u32[]{:S(2)}) copy-start(f32[384]{0:T(512)} %param.41) | copy-start | bytes 4612
  131.0 40.7 %copy-start.5 = (f32[512,384]{0,1:T(8,128)S(1)}, f32[512,384]{0,1:T(8,128)}, u32[]{:S(2)}) copy-start(f32[512,384]{0,1:T(8,128)} %convolution_add_fusion.13) | copy-start | bytes 2359300
  171.3 2.6 copy-start.30
  171.3 4.5 copy-start.43
  171.7 2.3 copy-start.13
  173.9 520.8 %reduce-scatter.3.cloned.1.call-start = ((), (), s32[]{:S(2)}) async-start(), calls=%async_computation.4 | async-start | bytes 2359296 | tf_op jit(solution)/shard_map/reduce_scatter | solution.py:165
  375.8 17.1 %copy-start.12 = (f32[512,384]{0,1:T(8,128)S(1)}, f32[512,384]{0,1:T(8,128)}, u32[]{:S(2)}) copy-start(f32[512,384]{0,1:T(8,128)} %convolution_add_fusion.11) | copy-start | bytes 2359300
  375.8 17.1 %copy-start.17 = (f32[512,128]{0,1:T(8,128)S(1)}, f32[512,128]{0,1:T(8,128)}, u32[]{:S(2)}) copy-start(f32[512,128]{0,1:T(8,128)} %copy.135) | copy-start | bytes 786436
  375.8 17.1 %copy-start.32 = (f32[512,128]{0,1:T(8,128)S(1)}, f32[512,128]{0,1:T(8,128)}, u32[]{:S(2)}) copy-start(f32[512,128]{0,1:T(8,128)} %get-tuple-element.713) | copy-start | bytes 786436
  389.5 4.3 copy-start.33
  392.9 1.4 copy-start.18
  392.9 1.4 copy-start.25
  392.9 1.0 copy-start.37
  422.7 2.9 copy-start.3
  435.5 2.9 copy-start.3
  448.2 2.9 copy-start.3
  461.0 2.9 copy-start.3
  473.8 2.9 copy-start.3
  486.6 2.9 copy-start.3
  499.4 2.9 copy-start.3
  512.2 2.9 copy-start.3
  525.0 2.9 copy-start.3
  537.8 2.9 copy-start.3
  550.6 2.9 copy-start.3
  563.4 2.9 copy-start.3
  576.2 2.9 copy-start.3
  589.0 2.9 copy-start.3
  601.8 2.9 copy-start.3
  614.5 2.9 copy-start.3
  653.3 79.1 %all-reduce.8.cloned.1.call-start = ((), (), s32[]{:S(2)}) async-start(), calls=%async_computation.5 | async-start | bytes 524288 | tf_op jit(solution)/shard_map/psum | solution.py:171
  694.7 297.9 %reduce-scatter.5.cloned.1.call-start = ((), (), s32[]{:S(2)}) async-start(), calls=%async_computation.6 | async-start | bytes 2359296 | tf_op jit(solution)/shard_map/reduce_scatter | solution.py:165
  732.4 3.2 copy-start.6
  732.4 4.4 copy-start.38
  735.6 1.7 copy-start.10
  735.6 1.7 copy-start.14
  919.1 5.3 copy-start.2
  948.5 3.3 copy-start.19
  948.5 3.3 copy-start.21
  948.5 3.3 copy-start.23
  948.5 3.3 copy-start.34
  951.4 1.6 copy-start.4
  951.5 86.6 %all-reduce.12.cloned.1.call-start = ((), (), s32[]{:S(2)}) async-start(), calls=%async_computation.8 | async-start | bytes 1048576 | tf_op jit(solution)/shard_map/psum | solution.py:171
  953.0 1.9 copy-start.28
  954.9 1.1 copy-start.31
  956.0 38.5 %copy-start.9 = (f32[512,128]{0,1:T(8,128)S(1)}, f32[512,128]{0,1:T(8,128)}, u32[]{:S(2)}) copy-start(f32[512,128]{0,1:T(8,128)} %copy-done.8) | copy-start | bytes 786436
  956.0 38.5 %copy-start.11 = (f32[512,128]{0,1:T(8,128)S(1)}, f32[512,128]{0,1:T(8,128)}, u32[]{:S(2)}) copy-start(f32[512,128]{0,1:T(8,128)} %copy-done.10) | copy-start | bytes 786436
  956.0 38.5 %copy-start.15 = (f32[512,128]{0,1:T(8,128)S(1)}, f32[512,128]{0,1:T(8,128)}, u32[]{:S(2)}) copy-start(f32[512,128]{0,1:T(8,128)} %copy-done.14) | copy-start | bytes 786436
  957.8 38.9 %copy-start.16 = (f32[512,128]{0,1:T(8,128)S(1)}, f32[512,128]{0,1:T(8,128)}, u32[]{:S(2)}) copy-start(f32[512,128]{0,1:T(8,128)} %get-tuple-element.704) | copy-start | bytes 786436
  992.6 110.7 %all-reduce.10.cloned.1.call-start = ((), (), s32[]{:S(2)}) async-start(), calls=%async_computation.7 | async-start | bytes 4980736 | tf_op jit(solution)/shard_map/psum | solution.py:182
  992.7 4.0 copy-start.26
  999.7 1.6 copy-start.29
  1001.1 37.0 %copy-start.24 = (f32[512,128]{0,1:T(8,128)S(1)}, f32[512,128]{0,1:T(8,128)}, u32[]{:S(2)}) copy-start(f32[512,128]{0,1:T(8,128)} %get-tuple-element.715) | copy-start | bytes 786436
  1038.1 65.3 %copy-start.39 = (f32[4096,16]{0,1:T(8,128)S(1)}, f32[4096,16]{0,1:T(8,128)}, u32[]{:S(2)}) copy-start(f32[4096,16]{0,1:T(8,128)} %get-tuple-element.1152) | copy-start | bytes 786436
  1104.0 3.2 copy-start.41
  1104.0 3.8 copy-start.40
  (3 other events, 2.2 us)
Sparse Core Ops, SparseCore 0:
  10.5 26.2 all-gather.2
  174.0 23.5 all-gather.4
  653.4 41.2 reduce-scatter.2
  697.0 35.3 all-reduce.7
  951.6 40.9 reduce-scatter.4
  995.5 38.6 all-reduce.11
  1039.4 63.9 all-reduce.9
where the time goes:
time: 1130 us; the launch traced here: 1120 us
  matrix products  320 us (28%)
  other arithmetic  306 us (27%)
  waiting for transfers between devices  214 us (19%)
  local copies, waits for them, and re-layouts  194 us (17%)
  blocking collectives  63.1 us (6%)
  between operations  15.8 us (1%)
    dot_general x64, matrix products, edge_matrices(): jnp.dot(hidden_low, second_weight, preferred_element_type=f32) + second_bias  93.7 us
    reduce_sum x32, other arithmetic, grad_block(): grad_bias = totals[1] + jnp.sum(outer_low.astype(f32), axis=0)  83.6 us
    reduce_scatter x2, waiting for transfers between devices, body(): lax.psum_scatter(spread(jnp.int32(0), node_rows * lax.axis_size('blk')),...  76.2 us
    dot_general x32, matrix products, grad_block(): jnp.dot(hidden_low.T, outer_low, preferred_element_type=f32)  63.2 us
    psum x1, waiting for transfers between devices, body(): lax.psum((grad_first_weight, grad_first_bias, second_totals[0], second_to...  62.9 us
    while x96, local copies, waits for them, and re-layouts  56 us
    scatter-add x2, other arithmetic, body(): jax.ops.segment_sum(messages.reshape(edge_rows, part_rows), target_local,...  54.2 us
    dot_general x32, matrix products, grad_block(): jnp.dot(outer_low, second_weight.T, preferred_element_type=f32)  51 us
  transfers between devices with their start and end apart: 7, of which 6 were waited for; matrix products, arithmetic and copies ran while one was open for 3% of the time, Pallas kernels for 0%

commit v1 on v0

v1 whole, which is shorter than its diff:
```python
import functools
from types import SimpleNamespace

import jax
import jax.numpy as jnp
from jax import lax
from jax.experimental import pallas as pl
from jax.experimental.pallas import tpu as pltpu
from jax.sharding import PartitionSpec as P

STEPS = 2
TILE = 512
LO = 256
ROWS = 512
F32, BF16, I32 = jnp.float32, jnp.bfloat16, jnp.int32
MESH = pl.DeviceIdType.MESH
VMEM = pl.BlockSpec(memory_space=pltpu.VMEM)

ROW_STATE_WEIGHT = 384
ROW_INPUT_BIAS = 768
ROW_STATE_BIAS = 776
ROW_FIRST = 784
ROW_SECOND_BIAS = 896
SMALL_ROWS = 1024

(P_STATE, P_STATE2, P_WEIGHT, P_SPREAD, P_SPREAD2, P_GRAD, P_GRAD_ALL, P_SMALL_ALL) = range(8)
(
    Z_WEIGHT,
    Z_BIAS,
    Z_SUM,
    Z_SUM2,
    Z_STATE,
    Z_FINAL,
    Z_DELTA,
    Z_DELTA2,
    Z_SOURCE,
    Z_SOURCE2,
    Z_GRADS,
    Z_FEATS,
    Z_FEATS_ALL,
    Z_SECOND,
    Z_SMALL,
) = range(15)


def nn(a, b):
    return jnp.dot(a, b, preferred_element_type=F32)


def nt(a, b):
    return lax.dot_general(a, b, (((1,), (1,)), ((), ())), preferred_element_type=F32)


def iota(shape, dim):
    return lax.broadcasted_iota(I32, shape, dim)


def ones_where(condition):
    return jnp.where(condition, 1.0, 0.0).astype(BF16)


def eye(n):
    return ones_where(iota((n, n), 0) == iota((n, n), 1))


def two(x):
    high = x.astype(BF16)
    return high, (x - high.astype(F32)).astype(BF16)


def three(x):
    high, rest = x.astype(BF16), x
    rest = x - high.astype(F32)
    mid = rest.astype(BF16)
    return high, mid, (rest - mid.astype(F32)).astype(BF16)


def nn2(a, x):
    high, low = two(x)
    return nn(a, high) + nn(a, low)


def nt2(x, b):
    high, low = two(x)
    return nt(high, b) + nt(low, b)


def sizes(mesh, edges, nodes, width):
    s = SimpleNamespace()
    s.B, s.R = mesh.shape["blk"], mesh.shape["rep"]
    s.E, s.N, s.H = edges, nodes, width
    s.J = width // s.R
    s.HIB = nodes // LO
    s.HI = s.HIB * s.B
    s.NQ = nodes // s.R
    s.EQ = edges // s.R
    s.OW = min(s.B, 8)
    s.STRIDE = s.B // s.OW
    s.T = s.J // s.OW
    s.KEEP = s.B <= 8
    s.SMALL = SMALL_ROWS // s.OW
    return s


def scratch(s):
    v = pltpu.VMEM
    jh = s.J * s.H
    shapes = dict(
        nst=v((s.H, s.N), F32),
        stq=v((STEPS, s.HIB, s.J, LO), BF16),
        tab=v((STEPS, s.B, s.HIB, s.J, LO), BF16),
        ys=v((s.R * s.T, s.J, s.H), F32),
        wsend=v((s.R, s.T, s.J, s.H), BF16),
        w2r=v((s.J, s.H, s.H), BF16),
        b2f=v((s.H, s.H), F32),
        baug=v((jh + SMALL_ROWS, s.H), BF16),
        w2k=v((s.H, jh), BF16),
        tl=v((1, s.E), I32),
        ohln=v((s.E, LO), BF16),
        mt=v((32, s.E), BF16),
        gm=v((16, s.E), BF16),
        ht=v((s.H, s.E), BF16),
        st=v((STEPS, s.J, s.E), BF16),
        smt=v((2 * s.H + s.J, s.N), F32),
        ssum=v((STEPS, s.J, s.N), F32),
        rsq=v((s.R, s.H, s.NQ), F32),
        rsl=v((STEPS, s.R, s.H, s.NQ), F32),
        keep=v((STEPS, 5, s.NQ, s.H), F32),
        keept=v((STEPS, 2, s.H, s.NQ), BF16),
        nsq=v((s.H, s.NQ), BF16),
        fin=v((s.NQ, s.H), F32),
        gq=v((STEPS, s.NQ, s.H), BF16),
        gfull=v((STEPS, s.N, s.H), BF16),
        gt=v((s.H, s.N), BF16),
        hg=v((s.H, s.E), F32),
        o=v((jh // 2, TILE), BF16),
        gacc=v((jh, s.H), F32),
        xs=v((ROWS, TILE), BF16),
        scat=v((s.HI * s.J, LO), F32),
        rps=v((s.B, s.HIB * s.J, LO), BF16),
        rpl=v((STEPS, s.B, s.HIB * s.J, LO), BF16),
        fzs=v((STEPS, s.R, s.J, s.NQ), F32),
        fzl=v((STEPS, s.R, s.J, s.NQ), F32),
        gradq=v((s.NQ, s.H), F32),
        small=v((SMALL_ROWS, s.H), F32),
        gland=v((s.B, jh // s.OW + s.SMALL, s.H), BF16),
        gz=v((s.R, s.T * s.J, s.H), BF16),
        sgz=v((s.R, s.SMALL, s.H), BF16),
        fqs=v((16, s.E), BF16),
        fql=v((s.R, 16, s.EQ), BF16),
        ps=pltpu.SemaphoreType.DMA((8, s.B)),
        pr=pltpu.SemaphoreType.DMA((8, s.B)),
        zs=pltpu.SemaphoreType.DMA((15, s.R)),
        zr=pltpu.SemaphoreType.DMA((15, s.R)),
        local=pltpu.SemaphoreType.DMA,
    )
    if not s.KEEP:
        shapes["gsend"] = v((jh + SMALL_ROWS, s.H), BF16)
    if s.KEEP:
        shapes["mat"] = v((jh, s.E), BF16)
    return shapes


IN_NAMES = (
    ["nodes", "feats", "src", "tgt", "grp", "cmask", "count", "w1", "b1"]
    + ["w2", "b2", "win", "wst", "bin", "bst", "cot"]
)
OUT_NAMES = ["final", "grads", "ff", "f", "sgf"]


def whole(s, names, *refs):
    c = SimpleNamespace(**dict(zip(names, refs)))
    B, R, H, J, E, N, NQ, EQ = s.B, s.R, s.H, s.J, s.E, s.N, s.NQ, s.EQ
    T, OW, STRIDE = s.T, s.OW, s.STRIDE
    jh = J * H
    tiles = E // TILE
    b = lax.axis_index("blk")
    r = lax.axis_index("rep")
    owner = b // STRIDE
    is_owner = lax.rem(b, STRIDE) == 0
    sent = []

    def push(src, dst, sems, rems, axis, peer):
        return pltpu.make_async_remote_copy(
            src_ref=src,
            dst_ref=dst,
            send_sem=sems,
            recv_sem=rems,
            device_id={axis: peer},
            device_id_type=MESH,
        )

    def plane(x, src_of, dst):
        copies = []
        for d in range(1, B):
            peer = lax.rem(b + d, B)
            cp = push(src_of(peer), dst, c.ps.at[x, d], c.pr.at[x, d], "blk", peer)
            cp.start()
            copies.append(cp)
        sent.extend(copies)
        return copies

    def line(x, src_of, dst):
        copies = []
        for d in range(1, R):
            peer = lax.rem(r + d, R)
            cp = push(src_of(peer), dst, c.zs.at[x, d], c.zr.at[x, d], "rep", peer)
            cp.start()
            copies.append(cp)
        sent.extend(copies)
        return copies

    def arrive(copies, reuse=False):
        for cp in copies:
            cp.wait_recv()
        if reuse:
            for cp in copies:
                cp.wait_send()
                sent[:] = [other for other in sent if other is not cp]

    def when_owner(fn):
        if STRIDE == 1:
            fn()
        else:
            pl.when(is_owner)(fn)

    def line_owner(x, src_of, dst):
        copies = []
        for d in range(1, R):
            peer = lax.rem(r + d, R)
            copies.append(push(src_of(peer), dst, c.zs.at[x, d], c.zr.at[x, d], "rep", peer))
        when_owner(lambda: [cp.start() for cp in copies] and None)
        owner_sent.extend(copies)
        return copies

    owner_sent = []

    def from_owners(x, src, dst_of):
        if STRIDE == 1:
            copies = plane(x, lambda peer: src, dst_of(owner))
            return lambda: arrive(copies)
        copies = []
        for d in range(1, B):
            peer = lax.rem(b + d, B)
            copies.append(push(src, dst_of(owner), c.ps.at[x, d], c.pr.at[x, owner], "blk", peer))
        when_owner(lambda: [cp.start() for cp in copies] and None)
        owner_sent.extend(copies)

        def wait():
            for q in range(OW):

                @pl.when(b != q * STRIDE)
                def _():
                    push(
                        src, dst_of(q), c.ps.at[x, 0], c.pr.at[x, q], "blk", lax.rem(b + 1, B)
                    ).wait_recv()

        return wait

    def to_owners(x, src_of, dst):
        if STRIDE == 1:
            copies = plane(x, src_of, dst)
            return lambda: arrive(copies)
        for q in range(OW):

            @pl.when(b != q * STRIDE)
            def _():
                push(src_of(q), dst, c.ps.at[x, q], c.pr.at[x, b], "blk", q * STRIDE).start()

        def wait():
            def arrivals():
                for d in range(1, B):
                    peer = lax.rem(b + d, B)
                    push(src_of(0), dst, c.ps.at[x, 0], c.pr.at[x, peer], "blk", peer).wait_recv()

            when_owner(arrivals)
            for q in range(OW):

                @pl.when(b != q * STRIDE)
                def _():
                    push(src_of(q), dst, c.ps.at[x, q], c.pr.at[x, b], "blk", q * STRIDE).wait_send()

        return wait

    def edges(t):
        return pl.ds(pl.multiple_of(t * TILE, TILE), TILE)

    barrier = pltpu.get_barrier_semaphore()
    for d in range(1, B):
        pl.semaphore_signal(
            barrier, inc=1, device_id={"blk": lax.rem(b + d, B)}, device_id_type=MESH
        )
    for d in range(1, R):
        pl.semaphore_signal(
            barrier, inc=1, device_id={"rep": lax.rem(r + d, R)}, device_id_type=MESH
        )

    weight_copy = pltpu.make_async_copy(c.w2, c.w2k, c.local)
    weight_copy.start()
    eye_h = eye(H)
    part = pl.ds(pl.multiple_of(r * J, J), J)

    c.nst[...] = c.nodes[...].T
    own_columns = c.nst[part, :].astype(BF16)
    for k in range(s.HIB):
        c.stq[0, k] = own_columns[:, k * LO : (k + 1) * LO]
    c.tab[0, b] = c.stq[0]
    row = iota((R * T, H), 0)
    pick = ones_where(iota((R * T, H), 1) == (row // T) * J + T * owner + lax.rem(row, T))
    weight_copy.wait()
    for i in range(J):
        c.ys[:, i, :] = nt(pick, c.w2k[:, i * H : (i + 1) * H])
    c.wsend[...] = c.ys[...].astype(BF16).reshape(R, T, J, H)
    pl.semaphore_wait(barrier, B - 1 + R - 1)

    states_in = plane(P_STATE, lambda peer: c.stq.at[0], c.tab.at[0, b])
    strip = pl.ds(pl.multiple_of(T * owner, T), T)
    weight_in = line_owner(Z_WEIGHT, lambda peer: c.wsend.at[peer], c.w2r.at[strip, part, :])
    c.b2f[part, :] = c.b2[...]
    bias_in = line(Z_BIAS, lambda peer: c.b2, c.b2f.at[part, :])

    def own_strip():
        c.w2r[strip, part, :] = c.wsend[r]

    when_owner(own_strip)

    place = iota((1, E), 1)
    c.tl[...] = jnp.where(place < c.count[...], c.tgt[...] - b * N, -1)
    cmt = nt(eye(16), c.cmask[...].astype(F32).astype(BF16)).astype(BF16)
    b1 = three(c.b1[...])
    first = jnp.concatenate(
        [c.w1[...].astype(F32)] + [x.astype(F32) for x in b1] + [jnp.zeros((13, H), F32)], axis=0
    ).astype(BF16)
    w1ta = nt(eye_h, first).astype(BF16)
    eye_t = eye(LO)

    def target_rows(t):
        return ones_where(iota((N, TILE), 0) == c.tl[:, edges(t)])

    def low_rows(t):
        return ones_where(iota((LO, TILE), 0) == (c.src[:, edges(t)] & (LO - 1)))

    def prepare(t, carry):
        e = edges(t)
        groups = ones_where(iota((16, TILE), 0) == c.grp[:, e])
        gm = nn(cmt, groups)
        c.gm[:, e] = gm.astype(BF16)
        masked = c.feats[:, e].astype(F32) * gm
        ones = jnp.where(iota((16, TILE), 0) < 3, 1.0, 0.0)
        mt = jnp.concatenate([masked, ones], axis=0).astype(BF16)
        c.mt[:, e] = mt
        pre = nn(w1ta, mt)
        c.ht[:, e] = (pre * jax.nn.sigmoid(pre)).astype(BF16)
        lows = low_rows(t)
        for k in range(TILE // LO):
            rows = pl.ds(pl.multiple_of(t * TILE + k * LO, LO), LO)
            c.ohln[rows, :] = nt(eye_t, lows[:, k * LO : (k + 1) * LO]).astype(BF16)
        return carry

    lax.fori_loop(0, tiles, prepare, 0)

    when_owner(lambda: arrive(weight_in))
    weight_wait = from_owners(
        P_WEIGHT,
        c.w2r.at[strip],
        lambda q: c.w2r.at[pl.ds(pl.multiple_of(T * q, T), T)],
    )

    def gather(step):
        def one(t, carry):
            e = edges(t)
            lows = low_rows(t)
            high = c.src[:, e] // LO
            total = jnp.zeros((J, TILE), F32)
            per = ROWS // J
            for g in range(s.HI // per):
                blocks = per // s.HIB
                table = c.tab[step, g * blocks : (g + 1) * blocks].reshape(ROWS, LO)
                rows = nn(table, lows)
                for k in range(per):
                    total = total + jnp.where(high == g * per + k, rows[k * J : (k + 1) * J], 0.0)
            c.st[step, :, e] = total.astype(BF16)
            return carry

        lax.fori_loop(0, tiles, one, 0)

    arrive(states_in)
    gather(0)

    arrive(bias_in)
    b2 = jnp.concatenate(three(c.b2f[...]), axis=1)

    def bias_columns(j, carry):
        at = iota((3 * H, H), 0)
        to = iota((3 * H, H), 1)
        move = ones_where((lax.rem(at, H) == r * J + j) & (to == at // H))
        c.baug[pl.ds(pl.multiple_of(j * H, H), H), :] = nn(b2, move).astype(BF16)
        return carry

    lax.fori_loop(0, J, bias_columns, 0)
    weight_wait()

    def turned(j, carry):
        c.w2k[:, pl.ds(pl.multiple_of(j * H, H), H)] = nt(eye_h, c.w2r[j]).astype(BF16)
        return carry

    lax.fori_loop(0, J, turned, 0)

    chunk = ROWS // H

    def hidden_rows(e):
        ones = jnp.where(iota((H, TILE), 0) < 3, 1.0, 0.0).astype(BF16)
        return jnp.concatenate([c.ht[:, e], ones], axis=0)

    def matrices(k, e, hidden, store):
        rows = slice(k * ROWS, (k + 1) * ROWS)
        if s.KEEP and not store:
            return c.mat[rows, e].astype(F32)
        left = jnp.concatenate(
            [c.w2r[k * chunk : (k + 1) * chunk].reshape(ROWS, H), c.baug[rows, :]], axis=1
        )
        low = nn(left, hidden).astype(BF16)
        if s.KEEP:
            c.mat[rows, e] = low
        return low.astype(F32)

    def messages(step):
        c.smt[...] = jnp.zeros_like(c.smt)

        def one(t, carry):
            e = edges(t)
            hidden = None if s.KEEP and step > 0 else hidden_rows(e)
            low = c.st[step, :, e]
            source = low.astype(F32)
            total = jnp.zeros((H, TILE), F32)
            for k in range(J // chunk):
                m = matrices(k, e, hidden, step == 0)
                for q in range(chunk):
                    j = k * chunk + q
                    total = total + m[q * H : (q + 1) * H] * source[j : j + 1, :]
            high, rest = two(total)
            rows = jnp.concatenate([high, rest, low], axis=0)
            c.smt[...] += nt(rows, target_rows(t))
            return carry

        lax.fori_loop(0, tiles, one, 0)
        summed = c.smt[0:H, :] + c.smt[H : 2 * H, :]
        c.ssum[step] = c.smt[2 * H : 2 * H + J, :]
        for q in range(R):
            c.rsq[q] = summed[:, q * NQ : (q + 1) * NQ]
        c.rsl[step, r] = c.rsq[r]
        return line(Z_SUM + step, lambda peer: c.rsq.at[peer], c.rsl.at[step, r])

    def gates(step, before, before_t):
        summed = c.rsl[step, 0]
        for q in range(1, R):
            summed = summed + c.rsl[step, q]
        summed_low = summed.T.astype(BF16)
        gi = nn(summed_low, c.win[...]) + c.bin[...]
        gs = nn(before.astype(BF16), c.wst[...]) + c.bst[...]
        reset = jax.nn.sigmoid(gi[:, :H] + gs[:, :H])
        update = jax.nn.sigmoid(gi[:, H : 2 * H] + gs[:, H : 2 * H])
        state_part = gs[:, 2 * H :]
        candidate = jnp.tanh(gi[:, 2 * H :] + reset * state_part)
        for k, x in enumerate((before, reset, update, candidate, state_part)):
            c.keep[step, k] = x
        c.keept[step, 0] = summed.astype(BF16)
        c.keept[step, 1] = before_t
        return (1.0 - update) * candidate + update * before

    nodes_here = pl.ds(pl.multiple_of(r * NQ, NQ), NQ)
    sums = messages(0)
    arrive(sums, reuse=True)
    state = gates(0, c.nodes[nodes_here, :], c.nst[:, nodes_here].astype(BF16))
    state_t = state.T.astype(BF16)
    c.nsq[...] = state_t
    hib = r // (LO // NQ)
    lanes = pl.ds(pl.multiple_of(lax.rem(r, LO // NQ) * NQ, NQ), NQ)
    c.stq[1, hib, :, lanes] = c.nsq[part, :]
    pieces = line(
        Z_STATE,
        lambda peer: c.nsq.at[pl.ds(pl.multiple_of(peer * J, J), J), :],
        c.stq.at[1, hib, :, lanes],
    )
    arrive(pieces)
    c.tab[1, b] = c.stq[1]
    arrive(plane(P_STATE2, lambda peer: c.stq.at[1], c.tab.at[1, b]))
    gather(1)
    sums = messages(1)
    arrive(sums)
    final = gates(1, state, state_t)
    c.fin[...] = final
    c.final[nodes_here, :] = final
    final_in = line(Z_FINAL, lambda peer: c.fin, c.final.at[nodes_here, :])

    c.small[...] = jnp.zeros_like(c.small)
    c.gacc[...] = jnp.zeros_like(c.gacc)

    def deltas(step, grad):
        before, reset, update, candidate, state_part = [c.keep[step, k] for k in range(5)]
        dn = grad * (1.0 - update)
        dz = grad * (before - candidate)
        dpn = dn * (1.0 - candidate * candidate)
        dpz = dz * update * (1.0 - update)
        dpr = dpn * state_part * reset * (1.0 - reset)
        to_input = jnp.concatenate([dpr, dpz, dpn], axis=1)
        to_state = jnp.concatenate([dpr, dpz, dpn * reset], axis=1)
        summed_grad = nt2(to_input, c.win[...]).astype(BF16)
        c.gq[step] = summed_grad
        c.gfull[step, nodes_here, :] = summed_grad
        copies = line(Z_DELTA + step, lambda peer: c.gq.at[step], c.gfull.at[step, nodes_here, :])
        gwi = nn2(c.keept[step, 0], to_input)
        gws = nn2(c.keept[step, 1], to_state)
        gbi = jnp.sum(to_input, axis=0, keepdims=True)
        gbs = jnp.sum(to_state, axis=0, keepdims=True)
        for k in range(3):
            cut = slice(k * H, (k + 1) * H)
            c.small[k * H : (k + 1) * H, :] += gwi[:, cut]
            c.small[ROW_STATE_WEIGHT + k * H : ROW_STATE_WEIGHT + (k + 1) * H, :] += gws[:, cut]
            c.small[ROW_INPUT_BIAS + k : ROW_INPUT_BIAS + k + 1, :] += gbi[:, cut]
            c.small[ROW_STATE_BIAS + k : ROW_STATE_BIAS + k + 1, :] += gbs[:, cut]
        c.gradq[...] = grad * update + nt2(to_state, c.wst[...])
        return copies

    def node_grads(step):
        c.gt[...] = nt(eye_h, c.gfull[step]).astype(BF16)
        rows = pl.ds(ROW_SECOND_BIAS + pl.multiple_of(r * J, J), J)
        high, low = two(c.ssum[step])
        c.small[rows, :] += nn(high, c.gfull[step]) + nn(low, c.gfull[step])

    def weights_tile(step, t):
        e = edges(t)
        at_edges = nn(c.gt[...], target_rows(t)).astype(BF16)
        source = c.st[step, :, e].astype(F32)
        got = None if step == STEPS - 1 else c.hg[:, e]
        half = J // 2
        for part_of in range(2):
            for q in range(half):
                j = part_of * half + q
                spread_row = jnp.broadcast_to(source[j : j + 1, :], (16, TILE)).astype(BF16)
                c.o[q * H : (q + 1) * H, :] = (
                    at_edges.reshape(H // 16, 16, TILE) * spread_row[None]
                ).reshape(H, TILE)
            base = part_of * half * H
            more = nn(c.w2k[:, base : base + half * H], c.o[...])
            got = more if got is None else got + more
            for k in range(half * H // ROWS):
                rows = slice(base + k * ROWS, base + (k + 1) * ROWS)
                c.gacc[rows, :] += nt(c.o[k * ROWS : (k + 1) * ROWS, :], c.ht[:, e])
        c.hg[:, e] = got

    def weights(step, begin, end):
        def one(t, carry):
            weights_tile(step, t)
            return carry

        lax.fori_loop(begin, end, one, 0)

    def sources(step):
        c.scat[...] = jnp.zeros_like(c.scat)

        def one(t, carry):
            e = edges(t)
            hidden = None if s.KEEP else hidden_rows(e)
            at_edges = nn(c.gt[...], target_rows(t))
            parts = []
            for k in range(J // chunk):
                m = matrices(k, e, hidden, False)
                for q in range(chunk):
                    parts.append(
                        jnp.sum(m[q * H : (q + 1) * H] * at_edges, axis=0, keepdims=True)
                    )
            got = jnp.concatenate(parts, axis=0)
            high = c.src[:, e] // LO
            per = ROWS // J
            for g in range(s.HI // per):
                for k in range(per):
                    c.xs[k * J : (k + 1) * J, :] = jnp.where(high == g * per + k, got, 0.0).astype(
                        BF16
                    )
                c.scat[g * ROWS : (g + 1) * ROWS, :] += nn(c.xs[...], c.ohln[e, :])
            return carry

        lax.fori_loop(0, tiles, one, 0)
        c.rps[...] = c.scat[...].astype(BF16).reshape(B, s.HIB * J, LO)
        c.rpl[step, b] = c.rps[b]
        return plane(P_SPREAD + step, lambda peer: c.rps.at[peer], c.rpl.at[step, b])

    def share_sources(step):
        total = c.rpl[step, 0].astype(F32)
        for q in range(1, B):
            total = total + c.rpl[step, q].astype(F32)
        for q in range(R):
            k, lane = (q * NQ) // LO, (q * NQ) % LO
            c.fzs[step, q] = total[k * J : (k + 1) * J, lane : lane + NQ]
        c.fzl[step, r] = c.fzs[step, r]
        return line(Z_SOURCE + step, lambda peer: c.fzs.at[step, peer], c.fzl.at[step, r])

    def state_grad(step):
        return c.gradq[...] + c.fzl[step].reshape(H, NQ).T

    last = STEPS - 1
    copies = deltas(last, c.cot[nodes_here, :])
    arrive(copies)
    node_grads(last)
    spread = sources(last)
    weights(last, 0, 3)
    arrive(spread, reuse=True)
    pieces = share_sources(last)
    weights(last, 3, 4)
    arrive(pieces)
    copies = deltas(0, state_grad(last))
    weights(last, 4, tiles)
    arrive(copies)
    node_grads(0)
    weights(0, 0, tiles)

    w1 = c.w1[...]

    def first_layer(t, carry):
        e = edges(t)
        mt = c.mt[:, e]
        pre = nn(w1ta, mt)
        gate = jax.nn.sigmoid(pre)
        pre_grad = c.hg[:, e] * gate * (1.0 + pre * (1.0 - gate))
        high, low = two(pre_grad)
        c.fqs[:, e] = ((nn(w1, high) + nn(w1, low)) * c.gm[:, e].astype(F32)).astype(BF16)
        c.small[ROW_FIRST : ROW_FIRST + 32, :] += nt(mt, high) + nt(mt, low)
        return carry

    lax.fori_loop(0, tiles, first_layer, 0)
    edges_here = pl.ds(pl.multiple_of(r * EQ, EQ), EQ)
    c.fql[r] = c.fqs[:, edges_here]
    feats_in = line(
        Z_FEATS,
        lambda peer: c.fqs.at[:, pl.ds(pl.multiple_of(peer * EQ, EQ), EQ)],
        c.fql.at[r],
    )

    per_owner = jh // OW
    piece = per_owner + s.SMALL
    outgoing = c.baug if s.KEEP else c.gsend
    for q in range(OW):
        at = q * piece
        outgoing[at : at + per_owner, :] = c.gacc[q * per_owner : (q + 1) * per_owner, :].astype(
            BF16
        )
        outgoing[at + per_owner : at + piece, :] = c.small[
            q * s.SMALL : (q + 1) * s.SMALL, :
        ].astype(BF16)

    def piece_of(q):
        return pl.ds(pl.multiple_of(q * piece, 16), piece)

    def own_grads():
        c.gland[b] = outgoing[piece_of(owner), :]

    when_owner(own_grads)
    grads_wait = to_owners(P_GRAD, lambda q: outgoing.at[piece_of(q), :], c.gland.at[b])

    spread = sources(0)

    grads_wait()

    def reduce_grads():
        for t in range(T):
            rows = slice(t * H, (t + 1) * H)
            total = c.gland[0, rows, :].astype(F32)
            for q in range(1, B):
                total = total + c.gland[q, rows, :].astype(F32)
            total = total.astype(BF16)
            for q in range(R):
                c.gz[q, t * J : (t + 1) * J, :] = total[q * J : (q + 1) * J, :]
        rows = slice(per_owner, per_owner + s.SMALL)
        total = c.gland[0, rows, :].astype(F32)
        for q in range(1, B):
            total = total + c.gland[q, rows, :].astype(F32)
        c.sgz[r] = total.astype(BF16)
        c.f[r, owner] = c.gz[r]

    when_owner(reduce_grads)
    second_in = line_owner(Z_SECOND, lambda peer: c.gz.at[peer], c.f.at[r, owner])
    small_in = line_owner(Z_SMALL, lambda peer: c.sgz.at[r], c.sgz.at[r])

    arrive(feats_in)
    feats = c.fql[0].astype(F32)
    for q in range(1, R):
        feats = feats + c.fql[q].astype(F32)
    c.ff[:, edges_here] = feats.astype(BF16)
    feats_all = line(Z_FEATS_ALL, lambda peer: c.ff.at[:, edges_here], c.ff.at[:, edges_here])

    arrive(spread)
    pieces = share_sources(0)

    when_owner(lambda: arrive(second_in))
    second_wait = from_owners(P_GRAD_ALL, c.f.at[:, owner], lambda q: c.f.at[:, q])

    def sum_small():
        arrive(small_in)
        total = c.sgz[0].astype(F32)
        for q in range(1, R):
            total = total + c.sgz[q].astype(F32)
        c.sgf[owner] = total.astype(BF16)

    when_owner(sum_small)
    small_wait = from_owners(P_SMALL_ALL, c.sgf.at[owner], lambda q: c.sgf.at[q])

    arrive(pieces)
    grad = state_grad(0)
    c.gradq[...] = grad
    c.grads[nodes_here, :] = grad
    grads_in = line(Z_GRADS, lambda peer: c.gradq, c.grads.at[nodes_here, :])

    arrive(feats_all)
    arrive(final_in)
    second_wait()
    small_wait()
    arrive(grads_in)
    for cp in sent:
        cp.wait_send()
    when_owner(lambda: [cp.wait_send() for cp in owner_sent] and None)


def finish(s, f_ref, ff_ref, sg_ref, feats_ref, w2_ref, win_ref, wst_ref, bin_ref, bst_ref, w1_ref, b1_ref, b2_ref, wide, turn):
    H, J = s.H, s.J
    wide[...] = f_ref[...].reshape(H * J, H).astype(F32)
    for i in range(J):
        w2_ref[:, i * H : (i + 1) * H] = wide[pl.ds(i, H, stride=J), :].T
    small = sg_ref[...].reshape(SMALL_ROWS, H).astype(F32)
    for k in range(3):
        cut = slice(k * H, (k + 1) * H)
        win_ref[:, cut] = small[k * H : (k + 1) * H]
        wst_ref[:, cut] = small[ROW_STATE_WEIGHT + k * H : ROW_STATE_WEIGHT + (k + 1) * H]
        bin_ref[:, cut] = small[ROW_INPUT_BIAS + k : ROW_INPUT_BIAS + k + 1]
        bst_ref[:, cut] = small[ROW_STATE_BIAS + k : ROW_STATE_BIAS + k + 1]
    w1_ref[...] = small[ROW_FIRST : ROW_FIRST + 16]
    b1_ref[...] = small[ROW_FIRST + 16 : ROW_FIRST + 17]
    turn[...] = small[ROW_SECOND_BIAS : ROW_SECOND_BIAS + H].T
    r = lax.axis_index("rep")
    b2_ref[...] = turn[pl.ds(pl.multiple_of(r * J, J), J), :]
    feats_ref[...] = ff_ref[...].astype(F32)


def body(
    s,
    node_states,
    edge_feats,
    edge_source,
    edge_target,
    edge_group,
    column_mask,
    edge_count,
    first_weight,
    first_bias,
    second_weight,
    second_bias,
    update_input_weight,
    update_state_weight,
    update_input_bias,
    update_state_bias,
    state_cotangent,
):
    H, N, E = s.H, s.N, s.E
    shapes = scratch(s)
    names = IN_NAMES + OUT_NAMES + list(shapes)
    sds = jax.ShapeDtypeStruct
    final, grads, ff, f, sgf = pl.pallas_call(
        functools.partial(whole, s, names),
        out_shape=[
            sds((N, H), F32),
            sds((N, H), F32),
            sds((16, E), BF16),
            sds((s.R, s.OW, s.T * s.J, H), BF16),
            sds((s.OW, s.SMALL, H), BF16),
        ],
        in_specs=[VMEM] * 9 + [pl.BlockSpec(memory_space=pl.ANY)] + [VMEM] * 6,
        out_specs=[VMEM] * 5,
        scratch_shapes=list(shapes.values()),
        compiler_params=pltpu.CompilerParams(
            collective_id=0, has_side_effects=True, vmem_limit_bytes=63 * 2**20
        ),
        name="edge_network",
    )(
        node_states,
        edge_feats.T,
        edge_source.reshape(1, E),
        edge_target.reshape(1, E),
        edge_group.reshape(1, E),
        column_mask,
        edge_count.reshape(1, 1),
        first_weight,
        first_bias.reshape(1, H),
        second_weight,
        second_bias.reshape(s.J, H),
        update_input_weight,
        update_state_weight,
        update_input_bias.reshape(1, 3 * H),
        update_state_bias.reshape(1, 3 * H),
        state_cotangent,
    )
    feats, w2, win, wst, bin_, bst, w1, b1, b2 = pl.pallas_call(
        functools.partial(finish, s),
        out_shape=[
            sds((16, E), F32),
            sds((H, s.J * H), F32),
            sds((H, 3 * H), F32),
            sds((H, 3 * H), F32),
            sds((1, 3 * H), F32),
            sds((1, 3 * H), F32),
            sds((16, H), F32),
            sds((1, H), F32),
            sds((s.J, H), F32),
        ],
        in_specs=[VMEM] * 3,
        out_specs=[VMEM] * 9,
        scratch_shapes=[pltpu.VMEM((H * s.J, H), F32), pltpu.VMEM((H, H), F32)],
        compiler_params=pltpu.CompilerParams(vmem_limit_bytes=32 * 2**20),
        name="finish",
    )(f, ff, sgf)
    return (
        final,
        grads,
        feats.T,
        w1,
        b1.reshape(-1),
        w2,
        b2.reshape(-1),
        win,
        wst,
        bin_.reshape(-1),
        bst.reshape(-1),
    )


def solution(mesh):
    in_specs = (
        P("blk", None),
        P("blk", None),
        P("blk"),
        P("blk"),
        P("blk"),
        P(),
        P("blk"),
        P(),
        P(),
        P(None, "rep"),
        P("rep"),
        P(),
        P(),
        P(),
        P(),
        P("blk", None),
    )
    out_specs = (
        P("blk", None),
        P("blk", None),
        P("blk", None),
        P(),
        P(),
        P(None, "rep"),
        P("rep"),
        P(),
        P(),
        P(),
        P(),
    )

    def run(*args):
        nodes, edges, width = args[0].shape[0], args[2].shape[0], args[0].shape[1]
        return body(sizes(mesh, edges, nodes, width), *args)

    return jax.shard_map(run, mesh=mesh, in_specs=in_specs, out_specs=out_specs, check_vma=False)
```

time: 1130 us -> 194 us (0.17); the launches traced: 1120 us -> 194 us
  matrix products: 320 us -> 0 us
  other arithmetic: 306 us -> 1.19 us
  waiting for transfers between devices: 214 us -> 0 us
  local copies, waits for them, and re-layouts: 194 us -> 7.94 us
  Pallas kernels: 0 us -> 183 us
  blocking collectives: 63.1 us -> 0 us
  between operations: 15.8 us -> 1.31 us
    dot_general x240 -> x0, matrix products: 320 us -> none  [the longest x64 93.7 us: edge_matrices(): jnp.dot(hidden_low, second_weight, preferred_element_type=f32) + second_bias]
    pallas_call x0 -> x2, Pallas kernels: none -> 183 us  [the longest x1 180 us: body(): pl.pallas_call(functools.partial(whole, s, names), out_shape=[sds((N, H),...]
    scatter-add x4 -> x0, other arithmetic: 102 us -> none  [the longest x2 54.2 us: body(): jax.ops.segment_sum(messages.reshape(edge_rows, part_rows), target_local,...]
    psum x3 -> x0, waiting for transfers between devices: 100 us -> none  [the longest x1 62.9 us: body(): lax.psum((grad_first_weight, grad_first_bias, second_totals[0], second_to...]
    reduce_sum x34 -> x0, other arithmetic: 85.1 us -> none  [the longest x32 83.6 us: grad_block(): grad_bias = totals[1] + jnp.sum(outer_low.astype(f32), axis=0)]
    reduce_scatter x2 -> x0, waiting for transfers between devices: 76.2 us -> none  [body(): lax.psum_scatter(spread(jnp.int32(0), node_rows * lax.axis_size('blk')),...]
    gather x4 -> x0, local copies, waits for them, and re-layouts: 57.9 us -> none  [the longest x2 29.9 us: body(): jnp.take(local_grad, target_local, axis=0).astype(f32) * live_edge[:, None]]
    while x96 -> x0, local copies, waits for them, and re-layouts: 56 us -> none
  transfers between devices with their start and end apart: 7 -> 0, of which waited for: 6 -> 0; matrix products, arithmetic and copies ran while one was open for 3% -> 0% of each run, Pallas kernels for 0% -> 0%
where the time goes in v1:
time: 194 us
  Pallas kernels  183 us (94%)
  local copies, waits for them, and re-layouts  7.94 us (4%)
    pallas_call x1, Pallas kernels, body(): pl.pallas_call(functools.partial(whole, s, names), out_shape=[sds((N, H),...  180 us
    unnamed x10, local copies, waits for them, and re-layouts  5.45 us

profile of v1, /device:TPU:0, one launch (start us, length us, event | category | flops | bytes accessed | tf_op | source)
XLA Modules:
  0.0 193.5 jit_solution(3281304377673446349)
XLA Ops:
  1.3 1.2 reshape.64.refs_13_
  2.5 1.2 reshape.65.refs_14_
  3.8 180.2 %edge_network.1 = (f32[512,128]{1,0:T(8,128)}, f32[512,128]{1,0:T(8,128)}, bf16[16,4096]{1,0:T(8,128)(2,1)}, bf16[4,8,128,128]{3,2,1,0:T(8,128)(2,1)}, bf16[8,128,128]{2,1,0:T(8,128)(2,1)}) custom-call(f32[512,128]{1,0:T(8,128)} %refs_0_.1, bf16[16,4096]{1,0:T(8,128)(2,1)} %bitcast.11, s32[1,4096]{1,0:T(1,128)} %bitcast.12, s32[1,4096]{1,0:T(1,128)} %bitcast.13, ...), custom_call_target="tpu_custom_call" | custom-call | tf_op jit(solution)/shard_map/edge_network/pallas_call | solution.py:767
  184.0 0.0 copy-start
  184.0 1.2 copy-done
  185.2 0.0 copy-start.1
  185.2 0.9 copy-done.1
  186.1 0.0 copy-start.2
  186.1 0.9 copy-done.2
  187.0 0.0 copy-start.3
  187.0 2.9 %finish.1 = (f32[16,4096]{1,0:T(8,128)}, f32[128,4096]{1,0:T(8,128)}, f32[128,384]{1,0:T(8,128)}, f32[128,384]{1,0:T(8,128)}, f32[1,384]{1,0:T(1,128)S(1)}, /*in...) custom-call(bf16[4,8,128,128]{3,2,1,0:T(8,128)(2,1)S(1)} %copy-done, ...), custom_call_target="tpu_custom_call" | custom-call | tf_op jit(solution)/shard_map/finish/pallas_call | solution.py:801
  189.9 0.6 reduce
  190.5 0.6 reduce.1
  191.1 1.7 copy.30
  192.8 0.0 copy-done.3
  192.8 0.7 copy.31
Async XLA Ops:
  184.0 1.2 copy-start
  185.2 0.9 copy-start.1
  186.1 0.9 copy-start.2
  187.0 5.8 %copy-start.3 = (f32[512,128]{1,0:T(8,128)S(1)}, f32[512,128]{1,0:T(8,128)}, u32[]{:S(2)}) copy-start(f32[512,128]{1,0:T(8,128)} %get-tuple-element.51) | copy-start | bytes 786436

commit v2 on v1

--- a/solution.py
+++ b/solution.py
@@ -12,6 +12,7 @@
 TILE = 512
 LO = 256
 ROWS = 512
+SLAB = 32
 F32, BF16, I32 = jnp.float32, jnp.bfloat16, jnp.int32
 MESH = pl.DeviceIdType.MESH
 VMEM = pl.BlockSpec(memory_space=pltpu.VMEM)
@@ -23,7 +24,20 @@
 ROW_SECOND_BIAS = 896
 SMALL_ROWS = 1024
 
-(P_STATE, P_STATE2, P_WEIGHT, P_SPREAD, P_SPREAD2, P_GRAD, P_GRAD_ALL, P_SMALL_ALL) = range(8)
+(
+    P_STATE,
+    P_STATE2,
+    P_WEIGHT,
+    P_WEIGHT_PAIR,
+    P_SPREAD,
+    P_SPREAD2,
+    P_GRAD_PAIR,
+    P_GRAD,
+    P_SMALL,
+    P_GRAD_ALL,
+    P_GRAD_ALL_PAIR,
+    PLANES,
+) = range(12)
 (
     Z_WEIGHT,
     Z_BIAS,
@@ -40,7 +54,8 @@
     Z_FEATS_ALL,
     Z_SECOND,
     Z_SMALL,
-) = range(15)
+    LINES,
+) = range(16)
 
 
 def nn(a, b):
@@ -99,6 +114,7 @@
     s.T = s.J // s.OW
     s.KEEP = s.B <= 8
     s.SMALL = SMALL_ROWS // s.OW
+    s.C = s.B // 2
     return s
 
 
@@ -113,7 +129,7 @@
         wsend=v((s.R, s.T, s.J, s.H), BF16),
         w2r=v((s.J, s.H, s.H), BF16),
         b2f=v((s.H, s.H), F32),
-        baug=v((jh + SMALL_ROWS, s.H), BF16),
+        baug=v((jh, s.H), BF16),
         w2k=v((s.H, jh), BF16),
         tl=v((1, s.E), I32),
         ohln=v((s.E, LO), BF16),
@@ -121,6 +137,8 @@
         gm=v((16, s.E), BF16),
         ht=v((s.H, s.E), BF16),
         st=v((STEPS, s.J, s.E), BF16),
+        sf=v((s.J, s.E), F32),
+        ge=v((s.H, s.E), BF16),
         smt=v((2 * s.H + s.J, s.N), F32),
         ssum=v((STEPS, s.J, s.N), F32),
         rsq=v((s.R, s.H, s.NQ), F32),
@@ -131,7 +149,6 @@
         fin=v((s.NQ, s.H), F32),
         gq=v((STEPS, s.NQ, s.H), BF16),
         gfull=v((STEPS, s.N, s.H), BF16),
-        gt=v((s.H, s.N), BF16),
         hg=v((s.H, s.E), F32),
         o=v((jh // 2, TILE), BF16),
         gacc=v((jh, s.H), F32),
@@ -142,20 +159,28 @@
         fzs=v((STEPS, s.R, s.J, s.NQ), F32),
         fzl=v((STEPS, s.R, s.J, s.NQ), F32),
         gradq=v((s.NQ, s.H), F32),
+        gradl=v((s.NQ, s.H), BF16),
         small=v((SMALL_ROWS, s.H), F32),
-        gland=v((s.B, jh // s.OW + s.SMALL, s.H), BF16),
+        sgsend=v((SMALL_ROWS, s.H), BF16),
+        sgland=v((s.B, s.SMALL, s.H), BF16),
         gz=v((s.R, s.T * s.J, s.H), BF16),
         sgz=v((s.R, s.SMALL, s.H), BF16),
         fqs=v((16, s.E), BF16),
         fql=v((s.R, 16, s.EQ), BF16),
-        ps=pltpu.SemaphoreType.DMA((8, s.B)),
-        pr=pltpu.SemaphoreType.DMA((8, s.B)),
-        zs=pltpu.SemaphoreType.DMA((15, s.R)),
-        zr=pltpu.SemaphoreType.DMA((15, s.R)),
+        ps=pltpu.SemaphoreType.DMA((PLANES, s.B)),
+        pr=pltpu.SemaphoreType.DMA((PLANES, s.B)),
+        zs=pltpu.SemaphoreType.DMA((LINES, s.R)),
+        zr=pltpu.SemaphoreType.DMA((LINES, s.R)),
         local=pltpu.SemaphoreType.DMA,
     )
-    if not s.KEEP:
-        shapes["gsend"] = v((jh + SMALL_ROWS, s.H), BF16)
+    piece = (jh // s.OW, s.H)
+    if s.STRIDE == 1:
+        shapes["gpair"] = v((s.C,) + piece, BF16)
+        shapes["gsum"] = v((s.C,) + piece, BF16)
+        shapes["gland"] = v((s.C,) + piece, BF16)
+    else:
+        shapes["gland"] = v((s.B,) + piece, BF16)
+        shapes["gsend"] = v((jh, s.H), BF16)
     if s.KEEP:
         shapes["mat"] = v((jh, s.E), BF16)
     return shapes
@@ -165,7 +190,7 @@
     ["nodes", "feats", "src", "tgt", "grp", "cmask", "count", "w1", "b1"]
     + ["w2", "b2", "win", "wst", "bin", "bst", "cot"]
 )
-OUT_NAMES = ["final", "grads", "ff", "f", "sgf"]
+OUT_NAMES = ["final", "grads", "ff", "f"]
 
 
 def whole(s, names, *refs):
@@ -235,14 +260,14 @@
 
     owner_sent = []
 
-    def from_owners(x, src, dst_of):
+    def from_owners(x, x2, strip_of):
         if STRIDE == 1:
-            copies = plane(x, lambda peer: src, dst_of(owner))
-            return lambda: arrive(copies)
+            return gather_pairs(x, x2, strip_of)
         copies = []
         for d in range(1, B):
             peer = lax.rem(b + d, B)
-            copies.append(push(src, dst_of(owner), c.ps.at[x, d], c.pr.at[x, owner], "blk", peer))
+            strip = strip_of(owner)
+            copies.append(push(strip, strip, c.ps.at[x, d], c.pr.at[x, owner], "blk", peer))
         when_owner(lambda: [cp.start() for cp in copies] and None)
         owner_sent.extend(copies)
 
@@ -251,11 +276,42 @@
 
                 @pl.when(b != q * STRIDE)
                 def _():
-                    push(
-                        src, dst_of(q), c.ps.at[x, 0], c.pr.at[x, q], "blk", lax.rem(b + 1, B)
-                    ).wait_recv()
-
-        return wait
+                    strip = strip_of(q)
+                    peer = lax.rem(b + 1, B)
+                    push(strip, strip, c.ps.at[x, 0], c.pr.at[x, q], "blk", peer).wait_recv()
+
+        return lambda: None, wait
+
+    chip, core = b // 2, lax.rem(b, 2)
+
+    def device(other, its_core):
+        return 2 * lax.rem(other, s.C) + its_core
+
+    def gather_pairs(x, x2, strip_of):
+        first, then = [], []
+        for m in range(1, s.C):
+            mine = strip_of(b)
+            first.append(
+                push(mine, mine, c.ps.at[x, m], c.pr.at[x, m], "blk", device(chip + m, core))
+            )
+        for m in range(s.C):
+            held = strip_of(device(chip + s.C - m, core))
+            then.append(
+                push(held, held, c.ps.at[x2, m], c.pr.at[x2, m], "blk", device(chip, 1 - core))
+            )
+        for cp in first + then[:1]:
+            cp.start()
+
+        def relay():
+            for m in range(1, s.C):
+                first[m - 1].wait_recv()
+                then[m].start()
+
+        def wait():
+            arrive(then)
+
+        sent.extend(first + then)
+        return relay, wait
 
     def to_owners(x, src_of, dst):
         if STRIDE == 1:
@@ -360,9 +416,9 @@
     lax.fori_loop(0, tiles, prepare, 0)
 
     when_owner(lambda: arrive(weight_in))
-    weight_wait = from_owners(
+    weight_relay, weight_wait = from_owners(
         P_WEIGHT,
-        c.w2r.at[strip],
+        P_WEIGHT_PAIR,
         lambda q: c.w2r.at[pl.ds(pl.multiple_of(T * q, T), T)],
     )
 
@@ -380,12 +436,14 @@
                 for k in range(per):
                     total = total + jnp.where(high == g * per + k, rows[k * J : (k + 1) * J], 0.0)
             c.st[step, :, e] = total.astype(BF16)
+            c.sf[:, e] = total
             return carry
 
         lax.fori_loop(0, tiles, one, 0)
 
     arrive(states_in)
     gather(0)
+    weight_relay()
 
     arrive(bias_in)
     b2 = jnp.concatenate(three(c.b2f[...]), axis=1)
@@ -397,14 +455,14 @@
         c.baug[pl.ds(pl.multiple_of(j * H, H), H), :] = nn(b2, move).astype(BF16)
         return carry
 
-    lax.fori_loop(0, J, bias_columns, 0)
+    lax.fori_loop(0, J, bias_columns, 0, unroll=8)
     weight_wait()
 
     def turned(j, carry):
         c.w2k[:, pl.ds(pl.multiple_of(j * H, H), H)] = nt(eye_h, c.w2r[j]).astype(BF16)
         return carry
 
-    lax.fori_loop(0, J, turned, 0)
+    lax.fori_loop(0, J, turned, 0, unroll=8)
 
     chunk = ROWS // H
 
@@ -412,10 +470,31 @@
         ones = jnp.where(iota((H, TILE), 0) < 3, 1.0, 0.0).astype(BF16)
         return jnp.concatenate([c.ht[:, e], ones], axis=0)
 
-    def matrices(k, e, hidden, store):
+    def held_messages(e):
+        parts = []
+        for k in range(H // SLAB):
+            total = jnp.zeros((SLAB, TILE), F32)
+            for j in range(J):
+                at = j * H + k * SLAB
+                total = total + c.mat[at : at + SLAB, e].astype(F32) * c.sf[j : j + 1, e]
+            parts.append(total)
+        return jnp.concatenate(parts, axis=0)
+
+    def held_sources(e):
+        grads = c.ge[:, e]
+        half, few = J // 2, H // 2
+        rows = iota((half, half * few), 0)
+        sums = ones_where(rows == iota((half, half * few), 1) // few)
+        parts = []
+        for k in range(2):
+            held = c.mat[k * half * H : (k + 1) * half * H, e].reshape(half, H, TILE)
+            product = held * grads[None]
+            product = product[:, :few] + product[:, few:]
+            parts.append(nn(sums, product.reshape(half * few, TILE)))
+        return jnp.concatenate(parts, axis=0)
+
+    def matrices(k, e, hidden):
         rows = slice(k * ROWS, (k + 1) * ROWS)
-        if s.KEEP and not store:
-            return c.mat[rows, e].astype(F32)
         left = jnp.concatenate(
             [c.w2r[k * chunk : (k + 1) * chunk].reshape(ROWS, H), c.baug[rows, :]], axis=1
         )
@@ -429,15 +508,18 @@
 
         def one(t, carry):
             e = edges(t)
-            hidden = None if s.KEEP and step > 0 else hidden_rows(e)
             low = c.st[step, :, e]
-            source = low.astype(F32)
-            total = jnp.zeros((H, TILE), F32)
-            for k in range(J // chunk):
-                m = matrices(k, e, hidden, step == 0)
-                for q in range(chunk):
-                    j = k * chunk + q
-                    total = total + m[q * H : (q + 1) * H] * source[j : j + 1, :]
+            if s.KEEP and step > 0:
+                total = held_messages(e)
+            else:
+                source = low.astype(F32)
+                hidden = hidden_rows(e)
+                total = jnp.zeros((H, TILE), F32)
+                for k in range(J // chunk):
+                    m = matrices(k, e, hidden)
+                    for q in range(chunk):
+                        j = k * chunk + q
+                        total = total + m[q * H : (q + 1) * H] * source[j : j + 1, :]
             high, rest = two(total)
             rows = jnp.concatenate([high, rest, low], axis=0)
             c.smt[...] += nt(rows, target_rows(t))
@@ -451,13 +533,16 @@
         c.rsl[step, r] = c.rsq[r]
         return line(Z_SUM + step, lambda peer: c.rsq.at[peer], c.rsl.at[step, r])
 
+    def gate_bias(ref):
+        return jnp.concatenate([ref[k : k + 1, :] for k in range(3)], axis=1)
+
     def gates(step, before, before_t):
         summed = c.rsl[step, 0]
         for q in range(1, R):
             summed = summed + c.rsl[step, q]
         summed_low = summed.T.astype(BF16)
-        gi = nn(summed_low, c.win[...]) + c.bin[...]
-        gs = nn(before.astype(BF16), c.wst[...]) + c.bst[...]
+        gi = nn(summed_low, c.win[...]) + gate_bias(c.bin)
+        gs = nn(before.astype(BF16), c.wst[...]) + gate_bias(c.bst)
         reset = jax.nn.sigmoid(gi[:, :H] + gs[:, :H])
         update = jax.nn.sigmoid(gi[:, H : 2 * H] + gs[:, H : 2 * H])
         state_part = gs[:, 2 * H :]
@@ -491,7 +576,6 @@
     final = gates(1, state, state_t)
     c.fin[...] = final
     c.final[nodes_here, :] = final
-    final_in = line(Z_FINAL, lambda peer: c.fin, c.final.at[nodes_here, :])
 
     c.small[...] = jnp.zeros_like(c.small)
     c.gacc[...] = jnp.zeros_like(c.gacc)
@@ -523,14 +607,20 @@
         return copies
 
     def node_grads(step):
-        c.gt[...] = nt(eye_h, c.gfull[step]).astype(BF16)
+        gt = nt(eye_h, c.gfull[step]).astype(BF16)
+
+        def one(t, carry):
+            c.ge[:, edges(t)] = nn(gt, target_rows(t)).astype(BF16)
+            return carry
+
+        lax.fori_loop(0, tiles, one, 0, unroll=2)
         rows = pl.ds(ROW_SECOND_BIAS + pl.multiple_of(r * J, J), J)
         high, low = two(c.ssum[step])
         c.small[rows, :] += nn(high, c.gfull[step]) + nn(low, c.gfull[step])
 
     def weights_tile(step, t):
         e = edges(t)
-        at_edges = nn(c.gt[...], target_rows(t)).astype(BF16)
+        at_edges = c.ge[:, e]
         source = c.st[step, :, e].astype(F32)
         got = None if step == STEPS - 1 else c.hg[:, e]
         half = J // 2
@@ -561,16 +651,19 @@
 
         def one(t, carry):
             e = edges(t)
-            hidden = None if s.KEEP else hidden_rows(e)
-            at_edges = nn(c.gt[...], target_rows(t))
-            parts = []
-            for k in range(J // chunk):
-                m = matrices(k, e, hidden, False)
-                for q in range(chunk):
-                    parts.append(
-                        jnp.sum(m[q * H : (q + 1) * H] * at_edges, axis=0, keepdims=True)
-                    )
-            got = jnp.concatenate(parts, axis=0)
+            if s.KEEP:
+                got = held_sources(e)
+            else:
+                at_edges = c.ge[:, e].astype(F32)
+                hidden = hidden_rows(e)
+                parts = []
+                for k in range(J // chunk):
+                    m = matrices(k, e, hidden)
+                    for q in range(chunk):
+                        parts.append(
+                            jnp.sum(m[q * H : (q + 1) * H] * at_edges, axis=0, keepdims=True)
+                        )
+                got = jnp.concatenate(parts, axis=0)
             high = c.src[:, e] // LO
             per = ROWS // J
             for g in range(s.HI // per):
@@ -602,6 +695,7 @@
     last = STEPS - 1
     copies = deltas(last, c.cot[nodes_here, :])
     arrive(copies)
+    final_in = line(Z_FINAL, lambda peer: c.fin, c.final.at[nodes_here, :])
     node_grads(last)
     spread = sources(last)
     weights(last, 0, 3)
@@ -615,6 +709,41 @@
     node_grads(0)
     weights(0, 0, tiles)
 
+    per_owner = jh // OW
+
+    def grad_rows(q):
+        return c.gacc[pl.ds(pl.multiple_of(q * per_owner, per_owner), per_owner), :]
+
+    if STRIDE == 1:
+        pair = []
+        for m in range(s.C):
+            rows = slice(m * per_owner, (m + 1) * per_owner)
+            c.baug[rows, :] = grad_rows(device(m, 1 - core)).astype(BF16)
+            x = P_GRAD_PAIR
+            cp = push(
+                c.baug.at[rows, :],
+                c.gpair.at[m],
+                c.ps.at[x, m],
+                c.pr.at[x, m],
+                "blk",
+                device(chip, 1 - core),
+            )
+            cp.start()
+            pair.append(cp)
+        sent.extend(pair)
+    else:
+        c.gsend[...] = c.gacc[...].astype(BF16)
+
+        def own_grads():
+            c.gland[b] = grad_rows(owner).astype(BF16)
+
+        when_owner(own_grads)
+        grads_wait = to_owners(
+            P_GRAD,
+            lambda q: c.gsend.at[pl.ds(pl.multiple_of(q * per_owner, per_owner), per_owner), :],
+            c.gland.at[b],
+        )
+
     w1 = c.w1[...]
 
     def first_layer(t, carry):
@@ -629,6 +758,35 @@
         return carry
 
     lax.fori_loop(0, tiles, first_layer, 0)
+
+    if STRIDE == 1:
+        across = []
+        for m in list(range(1, s.C)) + [0]:
+            other = lax.rem(chip + m, s.C)
+            pair_piece = c.gpair.at[other]
+            if m == 1:
+                arrive(pair)
+            total = grad_rows(device(other, core)) + pair_piece[...].astype(F32)
+            if m == 0:
+                c.gland[chip] = total.astype(BF16)
+                continue
+            c.gsum[m] = total.astype(BF16)
+            x = P_GRAD
+            cp = push(
+                c.gsum.at[m],
+                c.gland.at[chip],
+                c.ps.at[x, m],
+                c.pr.at[x, m],
+                "blk",
+                device(other, core),
+            )
+            cp.start()
+            across.append(cp)
+        sent.extend(across)
+
+        def grads_wait():
+            arrive(across)
+
     edges_here = pl.ds(pl.multiple_of(r * EQ, EQ), EQ)
     c.fql[r] = c.fqs[:, edges_here]
     feats_in = line(
@@ -637,108 +795,113 @@
         c.fql.at[r],
     )
 
-    per_owner = jh // OW
-    piece = per_owner + s.SMALL
-    outgoing = c.baug if s.KEEP else c.gsend
-    for q in range(OW):
-        at = q * piece
-        outgoing[at : at + per_owner, :] = c.gacc[q * per_owner : (q + 1) * per_owner, :].astype(
-            BF16
-        )
-        outgoing[at + per_owner : at + piece, :] = c.small[
-            q * s.SMALL : (q + 1) * s.SMALL, :
-        ].astype(BF16)
-
-    def piece_of(q):
-        return pl.ds(pl.multiple_of(q * piece, 16), piece)
-
-    def own_grads():
-        c.gland[b] = outgoing[piece_of(owner), :]
-
-    when_owner(own_grads)
-    grads_wait = to_owners(P_GRAD, lambda q: outgoing.at[piece_of(q), :], c.gland.at[b])
+    c.sgsend[...] = c.small[...].astype(BF16)
+
+    def small_rows(q):
+        return pl.ds(pl.multiple_of(q * s.SMALL, s.SMALL), s.SMALL)
+
+    def own_small():
+        c.sgland[b] = c.sgsend[small_rows(owner), :]
+
+    when_owner(own_small)
+    small_wait = to_owners(P_SMALL, lambda q: c.sgsend.at[small_rows(q), :], c.sgland.at[b])
 
     spread = sources(0)
+
+    def total_of(ref, rows, count):
+        total = ref[0, rows, :].astype(F32)
+        for q in range(1, count):
+            total = total + ref[q, rows, :].astype(F32)
+        return total
 
     grads_wait()
 
     def reduce_grads():
         for t in range(T):
-            rows = slice(t * H, (t + 1) * H)
-            total = c.gland[0, rows, :].astype(F32)
-            for q in range(1, B):
-                total = total + c.gland[q, rows, :].astype(F32)
+            total = total_of(c.gland, slice(t * H, (t + 1) * H), s.C if STRIDE == 1 else B)
             total = total.astype(BF16)
             for q in range(R):
                 c.gz[q, t * J : (t + 1) * J, :] = total[q * J : (q + 1) * J, :]
-        rows = slice(per_owner, per_owner + s.SMALL)
-        total = c.gland[0, rows, :].astype(F32)
-        for q in range(1, B):
-            total = total + c.gland[q, rows, :].astype(F32)
-        c.sgz[r] = total.astype(BF16)
         c.f[r, owner] = c.gz[r]
 
     when_owner(reduce_grads)
     second_in = line_owner(Z_SECOND, lambda peer: c.gz.at[peer], c.f.at[r, owner])
+    small_wait()
+
+    def reduce_small():
+        c.sgz[r] = total_of(c.sgland, slice(None), B).astype(BF16)
+
+    when_owner(reduce_small)
     small_in = line_owner(Z_SMALL, lambda peer: c.sgz.at[r], c.sgz.at[r])
 
     arrive(feats_in)
-    feats = c.fql[0].astype(F32)
-    for q in range(1, R):
-        feats = feats + c.fql[q].astype(F32)
-    c.ff[:, edges_here] = feats.astype(BF16)
+    c.ff[:, edges_here] = total_of(c.fql, slice(None), R).astype(BF16)
     feats_all = line(Z_FEATS_ALL, lambda peer: c.ff.at[:, edges_here], c.ff.at[:, edges_here])
 
     arrive(spread)
     pieces = share_sources(0)
 
-    when_owner(lambda: arrive(second_in))
-    second_wait = from_owners(P_GRAD_ALL, c.f.at[:, owner], lambda q: c.f.at[:, q])
-
     def sum_small():
         arrive(small_in)
-        total = c.sgz[0].astype(F32)
-        for q in range(1, R):
-            total = total + c.sgz[q].astype(F32)
-        c.sgf[owner] = total.astype(BF16)
+        c.f[R, owner] = total_of(c.sgz, slice(None), R).astype(BF16)
+        arrive(second_in)
 
     when_owner(sum_small)
-    small_wait = from_owners(P_SMALL_ALL, c.sgf.at[owner], lambda q: c.sgf.at[q])
+    second_relay, second_wait = from_owners(
+        P_GRAD_ALL, P_GRAD_ALL_PAIR, lambda q: c.f.at[:, q]
+    )
 
     arrive(pieces)
-    grad = state_grad(0)
-    c.gradq[...] = grad
+    grad = state_grad(0).astype(BF16)
+    c.gradl[...] = grad
     c.grads[nodes_here, :] = grad
-    grads_in = line(Z_GRADS, lambda peer: c.gradq, c.grads.at[nodes_here, :])
+    grads_in = line(Z_GRADS, lambda peer: c.gradl, c.grads.at[nodes_here, :])
 
     arrive(feats_all)
     arrive(final_in)
+    second_relay()
+    arrive(grads_in)
     second_wait()
-    small_wait()
-    arrive(grads_in)
     for cp in sent:
         cp.wait_send()
     when_owner(lambda: [cp.wait_send() for cp in owner_sent] and None)
 
 
-def finish(s, f_ref, ff_ref, sg_ref, feats_ref, w2_ref, win_ref, wst_ref, bin_ref, bst_ref, w1_ref, b1_ref, b2_ref, wide, turn):
+FINISH_NAMES = (
+    ["f", "ff", "final", "grads"]
+    + ["o_final", "o_grads", "feats", "w2", "win", "wst", "bin", "bst", "w1", "b1", "b2"]
+    + ["hf", "hff", "hgrads", "wide", "turn", "sems"]
+)
+
+
+def finish(s, *refs):
+    c = SimpleNamespace(**dict(zip(FINISH_NAMES, refs)))
     H, J = s.H, s.J
-    wide[...] = f_ref[...].reshape(H * J, H).astype(F32)
+    pairs = [(c.f, c.hf), (c.ff, c.hff), (c.grads, c.hgrads), (c.final, c.o_final)]
+    copies = [pltpu.make_async_copy(x, y, c.sems.at[k]) for k, (x, y) in enumerate(pairs)]
+    for cp in copies:
+        cp.start()
+    copies[0].wait()
+    c.wide[...] = c.hf[0 : s.R].reshape(H * J, H).astype(F32)
     for i in range(J):
-        w2_ref[:, i * H : (i + 1) * H] = wide[pl.ds(i, H, stride=J), :].T
-    small = sg_ref[...].reshape(SMALL_ROWS, H).astype(F32)
+        c.w2[:, i * H : (i + 1) * H] = c.wide[pl.ds(i, H, stride=J), :].T
+    small = c.hf[s.R].reshape(SMALL_ROWS, H).astype(F32)
     for k in range(3):
         cut = slice(k * H, (k + 1) * H)
-        win_ref[:, cut] = small[k * H : (k + 1) * H]
-        wst_ref[:, cut] = small[ROW_STATE_WEIGHT + k * H : ROW_STATE_WEIGHT + (k + 1) * H]
-        bin_ref[:, cut] = small[ROW_INPUT_BIAS + k : ROW_INPUT_BIAS + k + 1]
-        bst_ref[:, cut] = small[ROW_STATE_BIAS + k : ROW_STATE_BIAS + k + 1]
-    w1_ref[...] = small[ROW_FIRST : ROW_FIRST + 16]
-    b1_ref[...] = small[ROW_FIRST + 16 : ROW_FIRST + 17]
-    turn[...] = small[ROW_SECOND_BIAS : ROW_SECOND_BIAS + H].T
+        c.win[:, cut] = small[k * H : (k + 1) * H]
+        c.wst[:, cut] = small[ROW_STATE_WEIGHT + k * H : ROW_STATE_WEIGHT + (k + 1) * H]
+    c.bin[...] = small[ROW_INPUT_BIAS : ROW_INPUT_BIAS + 3]
+    c.bst[...] = small[ROW_STATE_BIAS : ROW_STATE_BIAS + 3]
+    c.w1[...] = small[ROW_FIRST : ROW_FIRST + 16]
+    c.b1[...] = small[ROW_FIRST + 16 : ROW_FIRST + 17]
+    c.turn[...] = small[ROW_SECOND_BIAS : ROW_SECOND_BIAS + H].T
     r = lax.axis_index("rep")
-    b2_ref[...] = turn[pl.ds(pl.multiple_of(r * J, J), J), :]
-    feats_ref[...] = ff_ref[...].astype(F32)
+    c.b2[...] = c.turn[pl.ds(pl.multiple_of(r * J, J), J), :]
+    copies[1].wait()
+    c.feats[...] = c.hff[...].astype(F32)
+    copies[2].wait()
+    c.o_grads[...] = c.hgrads[...].astype(F32)
+    copies[3].wait()
 
 
 def body(
@@ -764,17 +927,16 @@
     shapes = scratch(s)
     names = IN_NAMES + OUT_NAMES + list(shapes)
     sds = jax.ShapeDtypeStruct
-    final, grads, ff, f, sgf = pl.pallas_call(
+    final, grads, ff, f = pl.pallas_call(
         functools.partial(whole, s, names),
         out_shape=[
             sds((N, H), F32),
-            sds((N, H), F32),
+            sds((N, H), BF16),
             sds((16, E), BF16),
-            sds((s.R, s.OW, s.T * s.J, H), BF16),
-            sds((s.OW, s.SMALL, H), BF16),
+            sds((s.R + 1, s.OW, s.T * s.J, H), BF16),
         ],
         in_specs=[VMEM] * 9 + [pl.BlockSpec(memory_space=pl.ANY)] + [VMEM] * 6,
-        out_specs=[VMEM] * 5,
+        out_specs=[VMEM] * 4,
         scratch_shapes=list(shapes.values()),
         compiler_params=pltpu.CompilerParams(
             collective_id=0, has_side_effects=True, vmem_limit_bytes=63 * 2**20
@@ -794,29 +956,39 @@
         second_bias.reshape(s.J, H),
         update_input_weight,
         update_state_weight,
-        update_input_bias.reshape(1, 3 * H),
-        update_state_bias.reshape(1, 3 * H),
+        update_input_bias.reshape(3, H),
+        update_state_bias.reshape(3, H),
         state_cotangent,
     )
-    feats, w2, win, wst, bin_, bst, w1, b1, b2 = pl.pallas_call(
+    hbm = pl.BlockSpec(memory_space=pl.ANY)
+    final, grads, feats, w2, win, wst, bin_, bst, w1, b1, b2 = pl.pallas_call(
         functools.partial(finish, s),
         out_shape=[
+            sds((N, H), F32),
+            sds((N, H), F32),
             sds((16, E), F32),
             sds((H, s.J * H), F32),
             sds((H, 3 * H), F32),
             sds((H, 3 * H), F32),
-            sds((1, 3 * H), F32),
-            sds((1, 3 * H), F32),
+            sds((3, H), F32),
+            sds((3, H), F32),
             sds((16, H), F32),
             sds((1, H), F32),
             sds((s.J, H), F32),
         ],
-        in_specs=[VMEM] * 3,
-        out_specs=[VMEM] * 9,
-        scratch_shapes=[pltpu.VMEM((H * s.J, H), F32), pltpu.VMEM((H, H), F32)],
-        compiler_params=pltpu.CompilerParams(vmem_limit_bytes=32 * 2**20),
+        in_specs=[hbm] * 4,
+        out_specs=[hbm] + [VMEM] * 10,
+        scratch_shapes=[
+            pltpu.VMEM((s.R + 1, s.OW, s.T * s.J, H), BF16),
+            pltpu.VMEM((16, E), BF16),
+            pltpu.VMEM((N, H), BF16),
+            pltpu.VMEM((H * s.J, H), F32),
+            pltpu.VMEM((H, H), F32),
+            pltpu.SemaphoreType.DMA((4,)),
+        ],
+        compiler_params=pltpu.CompilerParams(vmem_limit_bytes=60 * 2**20),
         name="finish",
-    )(f, ff, sgf)
+    )(f, ff, final, grads)
     return (
         final,
         grads,

time: 194 us -> 162 us (0.84)
  Pallas kernels: 183 us -> 160 us
  local copies, waits for them, and re-layouts: 7.94 us -> 0 us
    pallas_call x1, Pallas kernels: 180 us -> 150 us  [body(): pl.pallas_call(functools.partial(whole, s, names), out_shape=[sds((N, H),...]
    pallas_call x1, Pallas kernels: 2.89 us -> 10.7 us  [body(): pl.pallas_call(functools.partial(finish, s), out_shape=[sds((N, H), F32),...]
    unnamed x10 -> x0, local copies, waits for them, and re-layouts: 5.45 us -> none
    reshape x2 -> x0, local copies, waits for them, and re-layouts: 2.49 us -> none  [the longest x1 1.25 us: body(): update_input_bias.reshape(1, 3 * H)]
where the time goes in v2:
time: 162 us
  Pallas kernels  160 us (99%)
    pallas_call x1, Pallas kernels, body(): pl.pallas_call(functools.partial(whole, s, names), out_shape=[sds((N, H),...  150 us
    pallas_call x1, Pallas kernels, body(): pl.pallas_call(functools.partial(finish, s), out_shape=[sds((N, H), F32),...  10.7 us

profile of v2, /device:TPU:0, one launch (start us, length us, event | category | flops | bytes accessed | tf_op | source)
XLA Modules:
  0.0 161.9 jit_solution(12247923435872966961)
XLA Ops:
  1.3 149.8 %edge_network.1 = (f32[512,128]{1,0:T(8,128)}, bf16[512,128]{1,0:T(8,128)(2,1)}, bf16[16,4096]{1,0:T(8,128)(2,1)}, bf16[5,8,128,128]{3,2,1,0:T(8,128)(2,1)}) custom-call(f32[512,128]{1,0:T(8,128)} %refs_0_.1, bf16[16,4096]{1,0:T(8,128)(2,1)} %bitcast.15, s32[1,4096]{1,0:T(1,128)} %bitcast.16, s32[1,4096]{1,0:T(1,128)} %bitcast.17, s32[1,4096]{1,0:T(1,128)} %bitcast.18, ...), custom_call_target="tpu_custom_call" | custom-call | tf_op jit(solution)/shard_map/edge_network/pallas_call | solution.py:930
  151.1 10.7 %finish.1 = (f32[512,128]{1,0:T(8,128)}, f32[512,128]{1,0:T(8,128)}, f32[16,4096]{1,0:T(8,128)}, f32[128,4096]{1,0:T(8,128)}, f32[128,384]{1,0:T(8,128)}, /*inde...) custom-call(bf16[5,8,128,128]{3,2,1,0:T(8,128)(2,1)} %get-tuple-elem, ...), custom_call_target="tpu_custom_call" | custom-call | tf_op jit(solution)/shard_map/finish/pallas_call | solution.py:964

commit v3 on v2

--- a/solution.py
+++ b/solution.py
@@ -13,6 +13,7 @@
 LO = 256
 ROWS = 512
 SLAB = 32
+VISITS = (22, 34)
 F32, BF16, I32 = jnp.float32, jnp.bfloat16, jnp.int32
 MESH = pl.DeviceIdType.MESH
 VMEM = pl.BlockSpec(memory_space=pltpu.VMEM)
@@ -20,7 +21,8 @@
 ROW_STATE_WEIGHT = 384
 ROW_INPUT_BIAS = 768
 ROW_STATE_BIAS = 776
-ROW_FIRST = 784
+GROUP = 16
+FIRST_ROWS = 32
 ROW_SECOND_BIAS = 896
 SMALL_ROWS = 1024
 
@@ -34,10 +36,11 @@
     P_GRAD_PAIR,
     P_GRAD,
     P_SMALL,
+    P_FIRST,
     P_GRAD_ALL,
     P_GRAD_ALL_PAIR,
     PLANES,
-) = range(12)
+) = range(13)
 (
     Z_WEIGHT,
     Z_BIAS,
@@ -54,8 +57,9 @@
     Z_FEATS_ALL,
     Z_SECOND,
     Z_SMALL,
+    Z_FIRST,
     LINES,
-) = range(16)
+) = range(17)
 
 
 def nn(a, b):
@@ -115,6 +119,8 @@
     s.KEEP = s.B <= 8
     s.SMALL = SMALL_ROWS // s.OW
     s.C = s.B // 2
+    s.G = nodes // GROUP
+    s.V = s.G + edges // LO
     return s
 
 
@@ -129,15 +135,16 @@
         wsend=v((s.R, s.T, s.J, s.H), BF16),
         w2r=v((s.J, s.H, s.H), BF16),
         b2f=v((s.H, s.H), F32),
-        baug=v((jh, s.H), BF16),
+        baug=v((s.J, s.H, s.H), BF16),
         w2k=v((s.H, jh), BF16),
         tl=v((1, s.E), I32),
         ohln=v((s.E, LO), BF16),
         mt=v((32, s.E), BF16),
         gm=v((16, s.E), BF16),
-        ht=v((s.H, s.E), BF16),
+        ht=v((s.E // LO, s.H, LO), BF16),
+        tlc=v((s.E // LO, 1, LO), I32),
         st=v((STEPS, s.J, s.E), BF16),
-        sf=v((s.J, s.E), F32),
+        sc=v((s.E // LO, s.J, LO), F32),
         ge=v((s.H, s.E), BF16),
         smt=v((2 * s.H + s.J, s.N), F32),
         ssum=v((STEPS, s.J, s.N), F32),
@@ -147,10 +154,9 @@
         keept=v((STEPS, 2, s.H, s.NQ), BF16),
         nsq=v((s.H, s.NQ), BF16),
         fin=v((s.NQ, s.H), F32),
-        gq=v((STEPS, s.NQ, s.H), BF16),
-        gfull=v((STEPS, s.N, s.H), BF16),
+        gq=v((STEPS, s.NQ // GROUP, GROUP, s.H), BF16),
+        gfull=v((STEPS, s.G, GROUP, s.H), BF16),
         hg=v((s.H, s.E), F32),
-        o=v((jh // 2, TILE), BF16),
         gacc=v((jh, s.H), F32),
         xs=v((ROWS, TILE), BF16),
         scat=v((s.HI * s.J, LO), F32),
@@ -161,6 +167,13 @@
         gradq=v((s.NQ, s.H), F32),
         gradl=v((s.NQ, s.H), BF16),
         small=v((SMALL_ROWS, s.H), F32),
+        q0=v((s.V, s.J * GROUP, s.H), BF16),
+        gv=v((s.V * GROUP, s.H), BF16),
+        planv=v((8, 128), I32),
+        plan=pltpu.SMEM((8, 128), I32),
+        firsts=v((FIRST_ROWS, s.H), F32),
+        flz=v((s.R, FIRST_ROWS, s.H), F32),
+        flp=v((s.B, FIRST_ROWS, s.H), F32),
         sgsend=v((SMALL_ROWS, s.H), BF16),
         sgland=v((s.B, s.SMALL, s.H), BF16),
         gz=v((s.R, s.T * s.J, s.H), BF16),
@@ -172,13 +185,10 @@
         zs=pltpu.SemaphoreType.DMA((LINES, s.R)),
         zr=pltpu.SemaphoreType.DMA((LINES, s.R)),
         local=pltpu.SemaphoreType.DMA,
+        ins=pltpu.SemaphoreType.DMA((len(IN_NAMES),)),
     )
     piece = (jh // s.OW, s.H)
-    if s.STRIDE == 1:
-        shapes["gpair"] = v((s.C,) + piece, BF16)
-        shapes["gsum"] = v((s.C,) + piece, BF16)
-        shapes["gland"] = v((s.C,) + piece, BF16)
-    else:
+    if s.STRIDE > 1:
         shapes["gland"] = v((s.B,) + piece, BF16)
         shapes["gsend"] = v((jh, s.H), BF16)
     if s.KEEP:
@@ -190,7 +200,7 @@
     ["nodes", "feats", "src", "tgt", "grp", "cmask", "count", "w1", "b1"]
     + ["w2", "b2", "win", "wst", "bin", "bst", "cot"]
 )
-OUT_NAMES = ["final", "grads", "ff", "f"]
+OUT_NAMES = ["final", "grads", "ff", "f", "fl"]
 
 
 def whole(s, names, *refs):
@@ -239,9 +249,12 @@
         for cp in copies:
             cp.wait_recv()
         if reuse:
-            for cp in copies:
-                cp.wait_send()
-                sent[:] = [other for other in sent if other is not cp]
+            release(copies)
+
+    def release(copies):
+        for cp in copies:
+            cp.wait_send()
+            sent[:] = [other for other in sent if other is not cp]
 
     def when_owner(fn):
         if STRIDE == 1:
@@ -280,7 +293,7 @@
                     peer = lax.rem(b + 1, B)
                     push(strip, strip, c.ps.at[x, 0], c.pr.at[x, q], "blk", peer).wait_recv()
 
-        return lambda: None, wait
+        return lambda: None, wait, [], []
 
     chip, core = b // 2, lax.rem(b, 2)
 
@@ -311,7 +324,7 @@
             arrive(then)
 
         sent.extend(first + then)
-        return relay, wait
+        return relay, wait, first, then
 
     def to_owners(x, src_of, dst):
         if STRIDE == 1:
@@ -351,11 +364,19 @@
             barrier, inc=1, device_id={"rep": lax.rem(r + d, R)}, device_id_type=MESH
         )
 
-    weight_copy = pltpu.make_async_copy(c.w2, c.w2k, c.local)
-    weight_copy.start()
+    loads = {}
+    for k, name in enumerate(IN_NAMES):
+        to = c.w2k if name == "w2" else getattr(c, name)
+        loads[name] = pltpu.make_async_copy(getattr(c, "in_" + name), to, c.ins.at[k])
+    for name in ["nodes", "w2"]:
+        loads[name].start()
+    for name in IN_NAMES:
+        if name not in ("nodes", "w2"):
+            loads[name].start()
     eye_h = eye(H)
     part = pl.ds(pl.multiple_of(r * J, J), J)
 
+    loads["nodes"].wait()
     c.nst[...] = c.nodes[...].T
     own_columns = c.nst[part, :].astype(BF16)
     for k in range(s.HIB):
@@ -363,10 +384,13 @@
     c.tab[0, b] = c.stq[0]
     row = iota((R * T, H), 0)
     pick = ones_where(iota((R * T, H), 1) == (row // T) * J + T * owner + lax.rem(row, T))
-    weight_copy.wait()
+    loads["w2"].wait()
     for i in range(J):
         c.ys[:, i, :] = nt(pick, c.w2k[:, i * H : (i + 1) * H])
     c.wsend[...] = c.ys[...].astype(BF16).reshape(R, T, J, H)
+    for name in IN_NAMES:
+        if name not in ("nodes", "w2"):
+            loads[name].wait()
     pl.semaphore_wait(barrier, B - 1 + R - 1)
 
     states_in = plane(P_STATE, lambda peer: c.stq.at[0], c.tab.at[0, b])
@@ -382,6 +406,17 @@
 
     place = iota((1, E), 1)
     c.tl[...] = jnp.where(place < c.count[...], c.tgt[...] - b * N, -1)
+    for k in range(E // LO):
+        c.tlc[k] = c.tl[:, k * LO : (k + 1) * LO]
+    ends = jnp.where(c.tgt[...] - b * N < GROUP * (iota((s.G, E), 0) + 1), 1, 0)
+    ends = jnp.sum(ends, axis=1, keepdims=True)
+    left_in = jnp.maximum((ends + (LO - 1)) // LO - 1, 0)
+    group = iota((s.G, 128), 0)
+    leave = group + jnp.where(group == s.G - 1, E // LO - 1, left_in)
+    visited = jnp.sum(jnp.where(leave < iota((s.G, 128), 1), 1, 0), axis=0, keepdims=True)
+    c.planv[...] = jnp.broadcast_to(visited, (8, 128))
+    plan_copy = pltpu.make_async_copy(c.planv, c.plan, c.local)
+    plan_copy.start()
     cmt = nt(eye(16), c.cmask[...].astype(F32).astype(BF16)).astype(BF16)
     b1 = three(c.b1[...])
     first = jnp.concatenate(
@@ -395,6 +430,19 @@
 
     def low_rows(t):
         return ones_where(iota((LO, TILE), 0) == (c.src[:, edges(t)] & (LO - 1)))
+
+    per_tile = TILE // LO
+
+    def put(ref, t, value):
+        for k in range(per_tile):
+            ref[t * per_tile + k] = value[:, k * LO : (k + 1) * LO]
+
+    def take(ref, t):
+        return jnp.concatenate([ref[t * per_tile + k] for k in range(per_tile)], axis=1)
+
+    def source_row(j, t):
+        rows = [c.sc[t * per_tile + k, j : j + 1, :] for k in range(per_tile)]
+        return jnp.concatenate(rows, axis=1)
 
     def prepare(t, carry):
         e = edges(t)
@@ -406,7 +454,7 @@
         mt = jnp.concatenate([masked, ones], axis=0).astype(BF16)
         c.mt[:, e] = mt
         pre = nn(w1ta, mt)
-        c.ht[:, e] = (pre * jax.nn.sigmoid(pre)).astype(BF16)
+        put(c.ht, t, (pre * jax.nn.sigmoid(pre)).astype(BF16))
         lows = low_rows(t)
         for k in range(TILE // LO):
             rows = pl.ds(pl.multiple_of(t * TILE + k * LO, LO), LO)
@@ -416,7 +464,7 @@
     lax.fori_loop(0, tiles, prepare, 0)
 
     when_owner(lambda: arrive(weight_in))
-    weight_relay, weight_wait = from_owners(
+    weight_relay, weight_wait, weight_chip, weight_pair = from_owners(
         P_WEIGHT,
         P_WEIGHT_PAIR,
         lambda q: c.w2r.at[pl.ds(pl.multiple_of(T * q, T), T)],
@@ -436,15 +484,13 @@
                 for k in range(per):
                     total = total + jnp.where(high == g * per + k, rows[k * J : (k + 1) * J], 0.0)
             c.st[step, :, e] = total.astype(BF16)
-            c.sf[:, e] = total
+            put(c.sc, t, total)
             return carry
 
         lax.fori_loop(0, tiles, one, 0)
 
     arrive(states_in)
     gather(0)
-    weight_relay()
-
     arrive(bias_in)
     b2 = jnp.concatenate(three(c.b2f[...]), axis=1)
 
@@ -452,31 +498,29 @@
         at = iota((3 * H, H), 0)
         to = iota((3 * H, H), 1)
         move = ones_where((lax.rem(at, H) == r * J + j) & (to == at // H))
-        c.baug[pl.ds(pl.multiple_of(j * H, H), H), :] = nn(b2, move).astype(BF16)
+        c.baug[j] = nn(b2, move).astype(BF16)
         return carry
 
     lax.fori_loop(0, J, bias_columns, 0, unroll=8)
-    weight_wait()
 
     def turned(j, carry):
         c.w2k[:, pl.ds(pl.multiple_of(j * H, H), H)] = nt(eye_h, c.w2r[j]).astype(BF16)
         return carry
 
-    lax.fori_loop(0, J, turned, 0, unroll=8)
-
     chunk = ROWS // H
 
-    def hidden_rows(e):
+    def hidden_rows(t):
         ones = jnp.where(iota((H, TILE), 0) < 3, 1.0, 0.0).astype(BF16)
-        return jnp.concatenate([c.ht[:, e], ones], axis=0)
-
-    def held_messages(e):
+        return jnp.concatenate([take(c.ht, t), ones], axis=0)
+
+    def held_messages(t):
+        e = edges(t)
         parts = []
         for k in range(H // SLAB):
             total = jnp.zeros((SLAB, TILE), F32)
             for j in range(J):
                 at = j * H + k * SLAB
-                total = total + c.mat[at : at + SLAB, e].astype(F32) * c.sf[j : j + 1, e]
+                total = total + c.mat[at : at + SLAB, e].astype(F32) * source_row(j, t)
             parts.append(total)
         return jnp.concatenate(parts, axis=0)
 
@@ -494,14 +538,31 @@
         return jnp.concatenate(parts, axis=0)
 
     def matrices(k, e, hidden):
-        rows = slice(k * ROWS, (k + 1) * ROWS)
+        cut = slice(k * chunk, (k + 1) * chunk)
         left = jnp.concatenate(
-            [c.w2r[k * chunk : (k + 1) * chunk].reshape(ROWS, H), c.baug[rows, :]], axis=1
+            [c.w2r[cut].reshape(ROWS, H), c.baug[cut].reshape(ROWS, H)], axis=1
         )
-        low = nn(left, hidden).astype(BF16)
-        if s.KEEP:
-            c.mat[rows, e] = low
-        return low.astype(F32)
+        return nn(left, hidden).astype(BF16).astype(F32)
+
+    def first_pass(strips, start):
+        def one(t, carry):
+            e = edges(t)
+            hidden = hidden_rows(t)
+            total = jnp.zeros((H, TILE), F32) if start else c.hg[:, e]
+            for q in strips:
+                cut = pl.ds(pl.multiple_of(q * T, T), T)
+                left = jnp.concatenate(
+                    [c.w2r[cut].reshape(T * H, H), c.baug[cut].reshape(T * H, H)], axis=1
+                )
+                low = nn(left, hidden).astype(BF16)
+                c.mat[pl.ds(pl.multiple_of(q * T * H, T * H), T * H), e] = low
+                m = low.astype(F32)
+                for p in range(T):
+                    total = total + m[p * H : (p + 1) * H] * source_row(q * T + p, t)
+            c.hg[:, e] = total
+            return carry
+
+        lax.fori_loop(0, tiles, one, 0)
 
     def messages(step):
         c.smt[...] = jnp.zeros_like(c.smt)
@@ -509,11 +570,11 @@
         def one(t, carry):
             e = edges(t)
             low = c.st[step, :, e]
-            if s.KEEP and step > 0:
-                total = held_messages(e)
+            if s.KEEP:
+                total = held_messages(t) if step > 0 else c.hg[:, e]
             else:
                 source = low.astype(F32)
-                hidden = hidden_rows(e)
+                hidden = hidden_rows(t)
                 total = jnp.zeros((H, TILE), F32)
                 for k in range(J // chunk):
                     m = matrices(k, e, hidden)
@@ -525,7 +586,7 @@
             c.smt[...] += nt(rows, target_rows(t))
             return carry
 
-        lax.fori_loop(0, tiles, one, 0)
+        lax.fori_loop(0, tiles, one, 0, unroll=2)
         summed = c.smt[0:H, :] + c.smt[H : 2 * H, :]
         c.ssum[step] = c.smt[2 * H : 2 * H + J, :]
         for q in range(R):
@@ -553,9 +614,37 @@
         c.keept[step, 1] = before_t
         return (1.0 - update) * candidate + update * before
 
+    def products(begin, end):
+        def one(t, carry):
+            g = c.plan[0, t]
+            ch = t - g
+            mine = ones_where(iota((GROUP, LO), 0) + g * GROUP == c.tlc[ch])
+            source = c.sc[ch]
+            parts = []
+            for j in range(J):
+                row = jnp.broadcast_to(source[j : j + 1, :], (GROUP, LO)).astype(BF16)
+                parts.append(row * mine)
+            c.q0[t] = nt(jnp.concatenate(parts, axis=0), c.ht[ch]).astype(BF16)
+            return carry
+
+        lax.fori_loop(begin, end, one, 0)
+
+    plan_copy.wait()
     nodes_here = pl.ds(pl.multiple_of(r * NQ, NQ), NQ)
+    groups_here = pl.ds(pl.multiple_of(r * (NQ // GROUP), NQ // GROUP), NQ // GROUP)
+    if s.KEEP:
+        weight_relay()
+        arrive(weight_pair)
+        half = OW // 2
+        first_pass(range(half), True)
+        first_pass(range(half, OW), False)
+    else:
+        weight_wait()
     sums = messages(0)
+    lax.fori_loop(0, J, turned, 0, unroll=8)
+    products(0, VISITS[0])
     arrive(sums, reuse=True)
+    release(weight_chip + weight_pair)
     state = gates(0, c.nodes[nodes_here, :], c.nst[:, nodes_here].astype(BF16))
     state_t = state.T.astype(BF16)
     c.nsq[...] = state_t
@@ -567,9 +656,12 @@
         lambda peer: c.nsq.at[pl.ds(pl.multiple_of(peer * J, J), J), :],
         c.stq.at[1, hib, :, lanes],
     )
+    products(VISITS[0], VISITS[1])
     arrive(pieces)
     c.tab[1, b] = c.stq[1]
-    arrive(plane(P_STATE2, lambda peer: c.stq.at[1], c.tab.at[1, b]))
+    states_in = plane(P_STATE2, lambda peer: c.stq.at[1], c.tab.at[1, b])
+    products(VISITS[1], s.V)
+    arrive(states_in)
     gather(1)
     sums = messages(1)
     arrive(sums)
@@ -590,9 +682,9 @@
         to_input = jnp.concatenate([dpr, dpz, dpn], axis=1)
         to_state = jnp.concatenate([dpr, dpz, dpn * reset], axis=1)
         summed_grad = nt2(to_input, c.win[...]).astype(BF16)
-        c.gq[step] = summed_grad
-        c.gfull[step, nodes_here, :] = summed_grad
-        copies = line(Z_DELTA + step, lambda peer: c.gq.at[step], c.gfull.at[step, nodes_here, :])
+        c.gq[step] = summed_grad.reshape(NQ // GROUP, GROUP, H)
+        c.gfull[step, groups_here] = c.gq[step]
+        copies = line(Z_DELTA + step, lambda peer: c.gq.at[step], c.gfull.at[step, groups_here])
         gwi = nn2(c.keept[step, 0], to_input)
         gws = nn2(c.keept[step, 1], to_state)
         gbi = jnp.sum(to_input, axis=0, keepdims=True)
@@ -607,7 +699,8 @@
         return copies
 
     def node_grads(step):
-        gt = nt(eye_h, c.gfull[step]).astype(BF16)
+        held = c.gfull[step].reshape(N, H)
+        gt = nt(eye_h, held).astype(BF16)
 
         def one(t, carry):
             c.ge[:, edges(t)] = nn(gt, target_rows(t)).astype(BF16)
@@ -616,38 +709,37 @@
         lax.fori_loop(0, tiles, one, 0, unroll=2)
         rows = pl.ds(ROW_SECOND_BIAS + pl.multiple_of(r * J, J), J)
         high, low = two(c.ssum[step])
-        c.small[rows, :] += nn(high, c.gfull[step]) + nn(low, c.gfull[step])
-
-    def weights_tile(step, t):
+        c.small[rows, :] += nn(high, held) + nn(low, held)
+
+    def weights_tile(step, t, second):
         e = edges(t)
         at_edges = c.ge[:, e]
         source = c.st[step, :, e].astype(F32)
         got = None if step == STEPS - 1 else c.hg[:, e]
-        half = J // 2
-        for part_of in range(2):
-            for q in range(half):
-                j = part_of * half + q
-                spread_row = jnp.broadcast_to(source[j : j + 1, :], (16, TILE)).astype(BF16)
-                c.o[q * H : (q + 1) * H, :] = (
-                    at_edges.reshape(H // 16, 16, TILE) * spread_row[None]
-                ).reshape(H, TILE)
-            base = part_of * half * H
-            more = nn(c.w2k[:, base : base + half * H], c.o[...])
+        spread = at_edges.reshape(H // 16, 16, TILE)
+        for k in range(jh // ROWS):
+            parts = []
+            for j in range(k * ROWS // H, (k + 1) * ROWS // H):
+                row = jnp.broadcast_to(source[j : j + 1, :], (16, TILE)).astype(BF16)
+                parts.append((spread * row[None]).reshape(H, TILE))
+            outer = jnp.concatenate(parts, axis=0)
+            rows = slice(k * ROWS, (k + 1) * ROWS)
+            more = nn(c.w2k[:, rows], outer)
             got = more if got is None else got + more
-            for k in range(half * H // ROWS):
-                rows = slice(base + k * ROWS, base + (k + 1) * ROWS)
-                c.gacc[rows, :] += nt(c.o[k * ROWS : (k + 1) * ROWS, :], c.ht[:, e])
+            if second:
+                c.gacc[rows, :] += nt(outer, take(c.ht, t))
         c.hg[:, e] = got
 
     def weights(step, begin, end):
         def one(t, carry):
-            weights_tile(step, t)
+            weights_tile(step, t, step == STEPS - 1)
             return carry
 
         lax.fori_loop(begin, end, one, 0)
 
-    def sources(step):
-        c.scat[...] = jnp.zeros_like(c.scat)
+    def sources(step, begin, end):
+        if begin == 0:
+            c.scat[...] = jnp.zeros_like(c.scat)
 
         def one(t, carry):
             e = edges(t)
@@ -655,7 +747,7 @@
                 got = held_sources(e)
             else:
                 at_edges = c.ge[:, e].astype(F32)
-                hidden = hidden_rows(e)
+                hidden = hidden_rows(t)
                 parts = []
                 for k in range(J // chunk):
                     m = matrices(k, e, hidden)
@@ -674,7 +766,9 @@
                 c.scat[g * ROWS : (g + 1) * ROWS, :] += nn(c.xs[...], c.ohln[e, :])
             return carry
 
-        lax.fori_loop(0, tiles, one, 0)
+        lax.fori_loop(begin, end, one, 0)
+
+    def spread_sources(step):
         c.rps[...] = c.scat[...].astype(BF16).reshape(B, s.HIB * J, LO)
         c.rpl[step, b] = c.rps[b]
         return plane(P_SPREAD + step, lambda peer: c.rps.at[peer], c.rpl.at[step, b])
@@ -697,17 +791,36 @@
     arrive(copies)
     final_in = line(Z_FINAL, lambda peer: c.fin, c.final.at[nodes_here, :])
     node_grads(last)
-    spread = sources(last)
+    sources(last, 0, tiles)
+    spread = spread_sources(last)
     weights(last, 0, 3)
     arrive(spread, reuse=True)
     pieces = share_sources(last)
-    weights(last, 3, 4)
+    weights(last, 3, 5)
     arrive(pieces)
     copies = deltas(0, state_grad(last))
-    weights(last, 4, tiles)
+    weights(last, 5, tiles)
     arrive(copies)
-    node_grads(0)
-    weights(0, 0, tiles)
+    def group_rows(t, carry):
+        rows = pl.ds(pl.multiple_of(t * GROUP, GROUP), GROUP)
+        c.gv[rows, :] = c.gfull[0, jnp.minimum(c.plan[0, t], s.G - 1)]
+        return carry
+
+    lax.fori_loop(0, s.V, group_rows, 0, unroll=8)
+    grads_t = nt(eye_h, c.gv[...]).astype(BF16)
+
+    def second_weight_rows(k, carry):
+        held = [
+            c.q0[:, pl.ds(pl.multiple_of((2 * k + p) * GROUP, GROUP), GROUP), :] for p in range(2)
+        ]
+        held = [x.reshape(s.V * GROUP, H) for x in held]
+        more = nn(grads_t, jnp.concatenate(held, axis=1))
+        for p in range(2):
+            rows = pl.ds(pl.multiple_of((2 * k + p) * H, H), H)
+            c.gacc[rows, :] += more[:, p * H : (p + 1) * H]
+        return carry
+
+    lax.fori_loop(0, J // 2, second_weight_rows, 0, unroll=4)
 
     per_owner = jh // OW
 
@@ -715,14 +828,19 @@
         return c.gacc[pl.ds(pl.multiple_of(q * per_owner, per_owner), per_owner), :]
 
     if STRIDE == 1:
+        def pieces_in(ref, first):
+            return lambda m: ref.at[pl.ds(pl.multiple_of((first + m) * T, T), T)]
+
+        from_pair, from_chip = pieces_in(c.w2r, 0), pieces_in(c.w2r, s.C)
+        to_pair, to_chip = pieces_in(c.baug, 0), pieces_in(c.baug, s.C)
         pair = []
         for m in range(s.C):
-            rows = slice(m * per_owner, (m + 1) * per_owner)
-            c.baug[rows, :] = grad_rows(device(m, 1 - core)).astype(BF16)
+            piece = grad_rows(device(m, 1 - core)).astype(BF16).reshape(T, H, H)
+            c.baug[m * T : (m + 1) * T] = piece
             x = P_GRAD_PAIR
             cp = push(
-                c.baug.at[rows, :],
-                c.gpair.at[m],
+                to_pair(m),
+                from_pair(m),
                 c.ps.at[x, m],
                 c.pr.at[x, m],
                 "blk",
@@ -744,7 +862,99 @@
             c.gland.at[b],
         )
 
+    node_grads(0)
+
+    c.sgsend[...] = c.small[...].astype(BF16)
+
+    def small_rows(q):
+        return pl.ds(pl.multiple_of(q * s.SMALL, s.SMALL), s.SMALL)
+
+    def own_small():
+        c.sgland[b] = c.sgsend[small_rows(owner), :]
+
+    when_owner(own_small)
+    small_wait = to_owners(P_SMALL, lambda q: c.sgsend.at[small_rows(q), :], c.sgland.at[b])
+
+    if STRIDE == 1:
+        across = []
+        for m in list(range(1, s.C)) + [0]:
+            other = lax.rem(chip + m, s.C)
+            if m == 1:
+                arrive(pair)
+            total = grad_rows(device(other, core)).reshape(T, H, H)
+            total = (total + from_pair(other)[...].astype(F32)).astype(BF16)
+            if m == 0:
+                c.w2r[pl.ds(pl.multiple_of((s.C + chip) * T, T), T)] = total
+                continue
+            c.baug[(s.C + m) * T : (s.C + m + 1) * T] = total
+            x = P_GRAD
+            cp = push(
+                to_chip(m),
+                from_chip(chip),
+                c.ps.at[x, m],
+                c.pr.at[x, m],
+                "blk",
+                device(other, core),
+            )
+            cp.start()
+            across.append(cp)
+        sent.extend(across)
+
+        def grads_wait():
+            arrive(across)
+
+    def total_of(ref, rows, count):
+        total = ref[0, rows, :].astype(F32)
+        for q in range(1, count):
+            total = total + ref[q, rows, :].astype(F32)
+        return total
+
+    sources(0, 0, tiles)
+    spread = spread_sources(0)
+    small_wait()
+
+    def reduce_small():
+        c.sgz[r] = total_of(c.sgland, slice(None), B).astype(BF16)
+
+    when_owner(reduce_small)
+    small_in = line_owner(Z_SMALL, lambda peer: c.sgz.at[r], c.sgz.at[r])
+    weights(0, 0, 2)
+    grads_wait()
+
+    def reduce_grads():
+        for t in range(T):
+            if STRIDE == 1:
+                total = c.w2r[s.C * T + t].astype(F32)
+                for q in range(1, s.C):
+                    total = total + c.w2r[(s.C + q) * T + t].astype(F32)
+            else:
+                total = total_of(c.gland, slice(t * H, (t + 1) * H), B)
+            total = total.astype(BF16)
+            for q in range(R):
+                c.gz[q, t * J : (t + 1) * J, :] = total[q * J : (q + 1) * J, :]
+        c.f[r, owner] = c.gz[r]
+
+    when_owner(reduce_grads)
+    second_in = line_owner(Z_SECOND, lambda peer: c.gz.at[peer], c.f.at[r, owner])
+    weights(0, 2, 5)
+    arrive(spread)
+    pieces = share_sources(0)
+    weights(0, 5, 7)
+
+    def sum_small():
+        arrive(small_in)
+        c.f[R, owner] = total_of(c.sgz, slice(None), R).astype(BF16)
+        arrive(second_in)
+
+    when_owner(sum_small)
+    second_relay, second_wait, _, _ = from_owners(
+        P_GRAD_ALL, P_GRAD_ALL_PAIR, lambda q: c.f.at[:, q]
+    )
+
+    weights(0, 7, tiles)
+
     w1 = c.w1[...]
+    c.firsts[...] = jnp.zeros_like(c.firsts)
 
     def first_layer(t, carry):
         e = edges(t)
@@ -754,39 +964,10 @@
         pre_grad = c.hg[:, e] * gate * (1.0 + pre * (1.0 - gate))
         high, low = two(pre_grad)
         c.fqs[:, e] = ((nn(w1, high) + nn(w1, low)) * c.gm[:, e].astype(F32)).astype(BF16)
-        c.small[ROW_FIRST : ROW_FIRST + 32, :] += nt(mt, high) + nt(mt, low)
+        c.firsts[...] += nt(mt, high) + nt(mt, low)
         return carry
 
     lax.fori_loop(0, tiles, first_layer, 0)
-
-    if STRIDE == 1:
-        across = []
-        for m in list(range(1, s.C)) + [0]:
-            other = lax.rem(chip + m, s.C)
-            pair_piece = c.gpair.at[other]
-            if m == 1:
-                arrive(pair)
-            total = grad_rows(device(other, core)) + pair_piece[...].astype(F32)
-            if m == 0:
-                c.gland[chip] = total.astype(BF16)
-                continue
-            c.gsum[m] = total.astype(BF16)
-            x = P_GRAD
-            cp = push(
-                c.gsum.at[m],
-                c.gland.at[chip],
-                c.ps.at[x, m],
-                c.pr.at[x, m],
-                "blk",
-                device(other, core),
-            )
-            cp.start()
-            across.append(cp)
-        sent.extend(across)
-
-        def grads_wait():
-            arrive(across)
-
     edges_here = pl.ds(pl.multiple_of(r * EQ, EQ), EQ)
     c.fql[r] = c.fqs[:, edges_here]
     feats_in = line(
@@ -794,62 +975,8 @@
         lambda peer: c.fqs.at[:, pl.ds(pl.multiple_of(peer * EQ, EQ), EQ)],
         c.fql.at[r],
     )
-
-    c.sgsend[...] = c.small[...].astype(BF16)
-
-    def small_rows(q):
-        return pl.ds(pl.multiple_of(q * s.SMALL, s.SMALL), s.SMALL)
-
-    def own_small():
-        c.sgland[b] = c.sgsend[small_rows(owner), :]
-
-    when_owner(own_small)
-    small_wait = to_owners(P_SMALL, lambda q: c.sgsend.at[small_rows(q), :], c.sgland.at[b])
-
-    spread = sources(0)
-
-    def total_of(ref, rows, count):
-        total = ref[0, rows, :].astype(F32)
-        for q in range(1, count):
-            total = total + ref[q, rows, :].astype(F32)
-        return total
-
-    grads_wait()
-
-    def reduce_grads():
-        for t in range(T):
-            total = total_of(c.gland, slice(t * H, (t + 1) * H), s.C if STRIDE == 1 else B)
-            total = total.astype(BF16)
-            for q in range(R):
-                c.gz[q, t * J : (t + 1) * J, :] = total[q * J : (q + 1) * J, :]
-        c.f[r, owner] = c.gz[r]
-
-    when_owner(reduce_grads)
-    second_in = line_owner(Z_SECOND, lambda peer: c.gz.at[peer], c.f.at[r, owner])
-    small_wait()
-
-    def reduce_small():
-        c.sgz[r] = total_of(c.sgland, slice(None), B).astype(BF16)
-
-    when_owner(reduce_small)
-    small_in = line_owner(Z_SMALL, lambda peer: c.sgz.at[r], c.sgz.at[r])
-
-    arrive(feats_in)
-    c.ff[:, edges_here] = total_of(c.fql, slice(None), R).astype(BF16)
-    feats_all = line(Z_FEATS_ALL, lambda peer: c.ff.at[:, edges_here], c.ff.at[:, edges_here])
-
-    arrive(spread)
-    pieces = share_sources(0)
-
-    def sum_small():
-        arrive(small_in)
-        c.f[R, owner] = total_of(c.sgz, slice(None), R).astype(BF16)
-        arrive(second_in)
-
-    when_owner(sum_small)
-    second_relay, second_wait = from_owners(
-        P_GRAD_ALL, P_GRAD_ALL_PAIR, lambda q: c.f.at[:, q]
-    )
+    c.flz[r] = c.firsts[...]
+    firsts_in = line(Z_FIRST, lambda peer: c.firsts, c.flz.at[r])
 
     arrive(pieces)
     grad = state_grad(0).astype(BF16)
@@ -857,10 +984,18 @@
     c.grads[nodes_here, :] = grad
     grads_in = line(Z_GRADS, lambda peer: c.gradl, c.grads.at[nodes_here, :])
 
-    arrive(feats_all)
-    arrive(final_in)
+    arrive(feats_in)
+    c.ff[:, edges_here] = total_of(c.fql, slice(None), R).astype(BF16)
+    feats_all = line(Z_FEATS_ALL, lambda peer: c.ff.at[:, edges_here], c.ff.at[:, edges_here])
+    arrive(firsts_in)
+    c.flp[b] = total_of(c.flz, slice(None), R)
+    firsts_all = plane(P_FIRST, lambda peer: c.flp.at[b], c.flp.at[b])
     second_relay()
     arrive(grads_in)
+    arrive(final_in)
+    arrive(firsts_all)
+    c.fl[...] = total_of(c.flp, slice(None), B)
+    arrive(feats_all)
     second_wait()
     for cp in sent:
         cp.wait_send()
@@ -868,9 +1003,9 @@
 
 
 FINISH_NAMES = (
-    ["f", "ff", "final", "grads"]
+    ["f", "ff", "final", "grads", "fl"]
     + ["o_final", "o_grads", "feats", "w2", "win", "wst", "bin", "bst", "w1", "b1", "b2"]
-    + ["hf", "hff", "hgrads", "wide", "turn", "sems"]
+    + ["hf", "hff", "hgrads", "hfl", "wide", "turn", "sems"]
 )
 
 
@@ -878,6 +1013,7 @@
     c = SimpleNamespace(**dict(zip(FINISH_NAMES, refs)))
     H, J = s.H, s.J
     pairs = [(c.f, c.hf), (c.ff, c.hff), (c.grads, c.hgrads), (c.final, c.o_final)]
+    pairs.append((c.fl, c.hfl))
     copies = [pltpu.make_async_copy(x, y, c.sems.at[k]) for k, (x, y) in enumerate(pairs)]
     for cp in copies:
         cp.start()
@@ -892,8 +1028,9 @@
         c.wst[:, cut] = small[ROW_STATE_WEIGHT + k * H : ROW_STATE_WEIGHT + (k + 1) * H]
     c.bin[...] = small[ROW_INPUT_BIAS : ROW_INPUT_BIAS + 3]
     c.bst[...] = small[ROW_STATE_BIAS : ROW_STATE_BIAS + 3]
-    c.w1[...] = small[ROW_FIRST : ROW_FIRST + 16]
-    c.b1[...] = small[ROW_FIRST + 16 : ROW_FIRST + 17]
+    copies[4].wait()
+    c.w1[...] = c.hfl[0:16]
+    c.b1[...] = c.hfl[16:17]
     c.turn[...] = small[ROW_SECOND_BIAS : ROW_SECOND_BIAS + H].T
     r = lax.axis_index("rep")
     c.b2[...] = c.turn[pl.ds(pl.multiple_of(r * J, J), J), :]
@@ -925,24 +1062,10 @@
 ):
     H, N, E = s.H, s.N, s.E
     shapes = scratch(s)
-    names = IN_NAMES + OUT_NAMES + list(shapes)
+    names = ["in_" + k for k in IN_NAMES] + OUT_NAMES + IN_NAMES + list(shapes)
     sds = jax.ShapeDtypeStruct
-    final, grads, ff, f = pl.pallas_call(
-        functools.partial(whole, s, names),
-        out_shape=[
-            sds((N, H), F32),
-            sds((N, H), BF16),
-            sds((16, E), BF16),
-            sds((s.R + 1, s.OW, s.T * s.J, H), BF16),
-        ],
-        in_specs=[VMEM] * 9 + [pl.BlockSpec(memory_space=pl.ANY)] + [VMEM] * 6,
-        out_specs=[VMEM] * 4,
-        scratch_shapes=list(shapes.values()),
-        compiler_params=pltpu.CompilerParams(
-            collective_id=0, has_side_effects=True, vmem_limit_bytes=63 * 2**20
-        ),
-        name="edge_network",
-    )(
+    hbm = pl.BlockSpec(memory_space=pl.ANY)
+    operands = (
         node_states,
         edge_feats.T,
         edge_source.reshape(1, E),
@@ -960,7 +1083,27 @@
         update_state_bias.reshape(3, H),
         state_cotangent,
     )
-    hbm = pl.BlockSpec(memory_space=pl.ANY)
+    held = [
+        pltpu.VMEM((8, 128) if name == "w2" else x.shape, F32 if name == "w2" else x.dtype)
+        for name, x in zip(IN_NAMES, operands)
+    ]
+    final, grads, ff, f, fl = pl.pallas_call(
+        functools.partial(whole, s, names),
+        out_shape=[
+            sds((N, H), F32),
+            sds((N, H), BF16),
+            sds((16, E), BF16),
+            sds((s.R + 1, s.OW, s.T * s.J, H), BF16),
+            sds((FIRST_ROWS, H), F32),
+        ],
+        in_specs=[hbm] * 16,
+        out_specs=[VMEM] * 5,
+        scratch_shapes=held + list(shapes.values()),
+        compiler_params=pltpu.CompilerParams(
+            collective_id=0, has_side_effects=True, vmem_limit_bytes=63 * 2**20
+        ),
+        name="edge_network",
+    )(*operands)
     final, grads, feats, w2, win, wst, bin_, bst, w1, b1, b2 = pl.pallas_call(
         functools.partial(finish, s),
         out_shape=[
@@ -976,19 +1119,20 @@
             sds((1, H), F32),
             sds((s.J, H), F32),
         ],
-        in_specs=[hbm] * 4,
-        out_specs=[hbm] + [VMEM] * 10,
+        in_specs=[hbm] * 5,
+        out_specs=[VMEM] * 11,
         scratch_shapes=[
             pltpu.VMEM((s.R + 1, s.OW, s.T * s.J, H), BF16),
             pltpu.VMEM((16, E), BF16),
             pltpu.VMEM((N, H), BF16),
+            pltpu.VMEM((FIRST_ROWS, H), F32),
             pltpu.VMEM((H * s.J, H), F32),
             pltpu.VMEM((H, H), F32),
-            pltpu.SemaphoreType.DMA((4,)),
+            pltpu.SemaphoreType.DMA((5,)),
         ],
         compiler_params=pltpu.CompilerParams(vmem_limit_bytes=60 * 2**20),
         name="finish",
-    )(f, ff, final, grads)
+    )(f, ff, final, grads, fl)
     return (
         final,
         grads,

time: 162 us -> 142 us (0.88)
  Pallas kernels: 160 us -> 140 us
    pallas_call x1, Pallas kernels: 150 us -> 136 us  [body(): pl.pallas_call(functools.partial(whole, s, names), out_shape=[sds((N, H),...]
    pallas_call x1, Pallas kernels: 10.7 us -> 4.59 us  [body(): pl.pallas_call(functools.partial(finish, s), out_shape=[sds((N, H), F32),...]
where the time goes in v3:
time: 142 us
  Pallas kernels  140 us (99%)
  between operations  1.46 us (1%)
    pallas_call x1, Pallas kernels, body(): pl.pallas_call(functools.partial(whole, s, names), out_shape=[sds((N, H),...  136 us
    pallas_call x1, Pallas kernels, body(): pl.pallas_call(functools.partial(finish, s), out_shape=[sds((N, H), F32),...  4.59 us

profile of v3, /device:TPU:0, one launch (start us, length us, event | category | flops | bytes accessed | tf_op | source)
XLA Modules:
  0.0 141.6 jit_solution(14240938117539180080)
XLA Ops:
  1.3 135.5 %edge_network.1 = (f32[512,128]{1,0:T(8,128)}, bf16[512,128]{1,0:T(8,128)(2,1)}, bf16[16,4096]{1,0:T(8,128)(2,1)}, bf16[5,8,128,128]{3,2,1,0:T(8,128)(2,1)}, f32[32,128]{1,0:T(8,128)}) custom-call(f32[512,128]{1,0:T(8,128)} %refs_0_.1, bf16[16,4096]{1,0:T(8,128)(2,1)} %bitcast.15, s32[1,4096]{1,0:T(1,128)} %bitcast.16, s32[1,4096]{1,0:T(1,128)} %bitcast.17, ...), custom_call_target="tpu_custom_call" | custom-call | tf_op jit(solution)/shard_map/edge_network/pallas_call | solution.py:1090
  136.8 4.6 %finish.1 = (f32[512,128]{1,0:T(8,128)}, f32[512,128]{1,0:T(8,128)}, f32[16,4096]{1,0:T(8,128)}, f32[128,4096]{1,0:T(8,128)}, f32[128,384]{1,0:T(8,128)}, /*inde...) custom-call(bf16[5,8,128,128]{3,2,1,0:T(8,128)(2,1)} %get-tuple-elem, ...), custom_call_target="tpu_custom_call" | custom-call | tf_op jit(solution)/shard_map/finish/pallas_call | solution.py:1107

commit v4 on v3

--- a/solution.py
+++ b/solution.py
@@ -14,6 +14,7 @@
 ROWS = 512
 SLAB = 32
 VISITS = (22, 34)
+NEAR = 2
 F32, BF16, I32 = jnp.float32, jnp.bfloat16, jnp.int32
 MESH = pl.DeviceIdType.MESH
 VMEM = pl.BlockSpec(memory_space=pltpu.VMEM)
@@ -144,7 +145,8 @@
         ht=v((s.E // LO, s.H, LO), BF16),
         tlc=v((s.E // LO, 1, LO), I32),
         st=v((STEPS, s.J, s.E), BF16),
-        sc=v((s.E // LO, s.J, LO), F32),
+        sf=v((s.J, s.E), F32),
+        sc=v((s.E // LO, s.J, LO), BF16),
         ge=v((s.H, s.E), BF16),
         smt=v((2 * s.H + s.J, s.N), F32),
         ssum=v((STEPS, s.J, s.N), F32),
@@ -193,6 +195,7 @@
         shapes["gsend"] = v((jh, s.H), BF16)
     if s.KEEP:
         shapes["mat"] = v((jh, s.E), BF16)
+        shapes["sums"] = v((2, s.J, jh // 4), BF16)
     return shapes
 
 
@@ -273,9 +276,7 @@
 
     owner_sent = []
 
-    def from_owners(x, x2, strip_of):
-        if STRIDE == 1:
-            return gather_pairs(x, x2, strip_of)
+    def from_owners(x, strip_of):
         copies = []
         for d in range(1, B):
             peer = lax.rem(b + d, B)
@@ -297,26 +298,38 @@
 
     chip, core = b // 2, lax.rem(b, 2)
 
-    def device(other, its_core):
-        return 2 * lax.rem(other, s.C) + its_core
-
-    def gather_pairs(x, x2, strip_of):
+    column, line_of = lax.rem(chip, 2), chip // 2
+    lines = max(s.C // 2, 1)
+
+    def device(m, its_core, back=False):
+        up = lines - m // 2 if back else m // 2
+        return 2 * (2 * lax.rem(line_of + up, lines) + lax.rem(column + lax.rem(m, 2), 2)) + its_core
+
+    def slot_rows(at):
+        if STRIDE > 1:
+            return at
+        slot = at // T
+        held_by = jnp.where(slot < s.C, core, 1 - core)
+        return T * device(lax.rem(slot, s.C), held_by, True) + lax.rem(at, T)
+
+    def slot(k):
+        return c.w2r.at[k * T : (k + 1) * T]
+
+    def gather_pairs(x, x2, first_of, then_of, late=s.C):
         first, then = [], []
         for m in range(1, s.C):
-            mine = strip_of(b)
-            first.append(
-                push(mine, mine, c.ps.at[x, m], c.pr.at[x, m], "blk", device(chip + m, core))
+            src, dst = first_of(m)
+            first.append(push(src, dst, c.ps.at[x, m], c.pr.at[x, m], "blk", device(m, core)))
+        for m in range(s.C):
+            src, dst = then_of(m)
+            then.append(
+                push(src, dst, c.ps.at[x2, m], c.pr.at[x2, m], "blk", device(0, 1 - core))
             )
-        for m in range(s.C):
-            held = strip_of(device(chip + s.C - m, core))
-            then.append(
-                push(held, held, c.ps.at[x2, m], c.pr.at[x2, m], "blk", device(chip, 1 - core))
-            )
-        for cp in first + then[:1]:
+        for cp in first[:late] + then[:1]:
             cp.start()
 
-        def relay():
-            for m in range(1, s.C):
+        def relay(begin=1, end=s.C):
+            for m in range(begin, end):
                 first[m - 1].wait_recv()
                 then[m].start()
 
@@ -394,7 +407,7 @@
     pl.semaphore_wait(barrier, B - 1 + R - 1)
 
     states_in = plane(P_STATE, lambda peer: c.stq.at[0], c.tab.at[0, b])
-    strip = pl.ds(pl.multiple_of(T * owner, T), T)
+    strip = pl.ds(0 if STRIDE == 1 else pl.multiple_of(T * owner, T), T)
     weight_in = line_owner(Z_WEIGHT, lambda peer: c.wsend.at[peer], c.w2r.at[strip, part, :])
     c.b2f[part, :] = c.b2[...]
     bias_in = line(Z_BIAS, lambda peer: c.b2, c.b2f.at[part, :])
@@ -437,12 +450,8 @@
         for k in range(per_tile):
             ref[t * per_tile + k] = value[:, k * LO : (k + 1) * LO]
 
-    def take(ref, t):
-        return jnp.concatenate([ref[t * per_tile + k] for k in range(per_tile)], axis=1)
-
-    def source_row(j, t):
-        rows = [c.sc[t * per_tile + k, j : j + 1, :] for k in range(per_tile)]
-        return jnp.concatenate(rows, axis=1)
+    def hidden_of(t):
+        return jnp.concatenate([c.ht[t * per_tile + k] for k in range(per_tile)], axis=1)
 
     def prepare(t, carry):
         e = edges(t)
@@ -454,7 +463,8 @@
         mt = jnp.concatenate([masked, ones], axis=0).astype(BF16)
         c.mt[:, e] = mt
         pre = nn(w1ta, mt)
-        put(c.ht, t, (pre * jax.nn.sigmoid(pre)).astype(BF16))
+        hidden = (pre * jax.nn.sigmoid(pre)).astype(BF16)
+        put(c.ht, t, hidden)
         lows = low_rows(t)
         for k in range(TILE // LO):
             rows = pl.ds(pl.multiple_of(t * TILE + k * LO, LO), LO)
@@ -464,13 +474,27 @@
     lax.fori_loop(0, tiles, prepare, 0)
 
     when_owner(lambda: arrive(weight_in))
-    weight_relay, weight_wait, weight_chip, weight_pair = from_owners(
-        P_WEIGHT,
-        P_WEIGHT_PAIR,
-        lambda q: c.w2r.at[pl.ds(pl.multiple_of(T * q, T), T)],
-    )
+    if STRIDE == 1:
+        weight_relay, weight_wait, weight_chip, weight_pair = gather_pairs(
+            P_WEIGHT,
+            P_WEIGHT_PAIR,
+            lambda m: (slot(0), slot(m)),
+            lambda m: (slot(m), slot(s.C + m)),
+        )
+    else:
+        weight_relay, weight_wait, weight_chip, weight_pair = from_owners(
+            P_WEIGHT, lambda q: c.w2r.at[pl.ds(pl.multiple_of(T * q, T), T)]
+        )
+
+    to_slots = ones_where(iota((J, J), 1) == slot_rows(iota((J, J), 0)))
+    from_slots = ones_where(iota((J, J), 0) == slot_rows(iota((J, J), 1)))
 
     def gather(step):
+        if STRIDE == 1:
+            for q in range(B):
+                for k in range(s.HIB):
+                    c.tab[step, q, k] = nn(to_slots, c.tab[step, q, k]).astype(BF16)
+
         def one(t, carry):
             e = edges(t)
             lows = low_rows(t)
@@ -484,7 +508,9 @@
                 for k in range(per):
                     total = total + jnp.where(high == g * per + k, rows[k * J : (k + 1) * J], 0.0)
             c.st[step, :, e] = total.astype(BF16)
-            put(c.sc, t, total)
+            c.sf[:, e] = total
+            if step == 0:
+                put(c.sc, t, total.astype(BF16))
             return carry
 
         lax.fori_loop(0, tiles, one, 0)
@@ -497,7 +523,7 @@
     def bias_columns(j, carry):
         at = iota((3 * H, H), 0)
         to = iota((3 * H, H), 1)
-        move = ones_where((lax.rem(at, H) == r * J + j) & (to == at // H))
+        move = ones_where((lax.rem(at, H) == r * J + slot_rows(j)) & (to == at // H))
         c.baug[j] = nn(b2, move).astype(BF16)
         return carry
 
@@ -511,7 +537,7 @@
 
     def hidden_rows(t):
         ones = jnp.where(iota((H, TILE), 0) < 3, 1.0, 0.0).astype(BF16)
-        return jnp.concatenate([take(c.ht, t), ones], axis=0)
+        return jnp.concatenate([hidden_of(t), ones], axis=0)
 
     def held_messages(t):
         e = edges(t)
@@ -520,22 +546,25 @@
             total = jnp.zeros((SLAB, TILE), F32)
             for j in range(J):
                 at = j * H + k * SLAB
-                total = total + c.mat[at : at + SLAB, e].astype(F32) * source_row(j, t)
+                total = total + c.mat[at : at + SLAB, e].astype(F32) * c.sf[j : j + 1, e]
             parts.append(total)
         return jnp.concatenate(parts, axis=0)
 
+    half, few = J // 2, H // 2
+    if s.KEEP:
+        rows, columns = iota((J, half * few), 0), iota((J, half * few), 1) // few
+        for k in range(2):
+            c.sums[k] = ones_where(rows == slot_rows(columns + k * half))
+
     def held_sources(e):
         grads = c.ge[:, e]
-        half, few = J // 2, H // 2
-        rows = iota((half, half * few), 0)
-        sums = ones_where(rows == iota((half, half * few), 1) // few)
-        parts = []
+        total = jnp.zeros((J, TILE), F32)
         for k in range(2):
             held = c.mat[k * half * H : (k + 1) * half * H, e].reshape(half, H, TILE)
             product = held * grads[None]
             product = product[:, :few] + product[:, few:]
-            parts.append(nn(sums, product.reshape(half * few, TILE)))
-        return jnp.concatenate(parts, axis=0)
+            total = total + nn(c.sums[k], product.reshape(half * few, TILE))
+        return total
 
     def matrices(k, e, hidden):
         cut = slice(k * chunk, (k + 1) * chunk)
@@ -550,19 +579,19 @@
             hidden = hidden_rows(t)
             total = jnp.zeros((H, TILE), F32) if start else c.hg[:, e]
             for q in strips:
-                cut = pl.ds(pl.multiple_of(q * T, T), T)
+                cut = slice(q * T, (q + 1) * T)
                 left = jnp.concatenate(
                     [c.w2r[cut].reshape(T * H, H), c.baug[cut].reshape(T * H, H)], axis=1
                 )
                 low = nn(left, hidden).astype(BF16)
-                c.mat[pl.ds(pl.multiple_of(q * T * H, T * H), T * H), e] = low
+                c.mat[q * T * H : (q + 1) * T * H, e] = low
                 m = low.astype(F32)
                 for p in range(T):
-                    total = total + m[p * H : (p + 1) * H] * source_row(q * T + p, t)
+                    total = total + m[p * H : (p + 1) * H] * c.sf[q * T + p : q * T + p + 1, e]
             c.hg[:, e] = total
             return carry
 
-        lax.fori_loop(0, tiles, one, 0)
+        lax.fori_loop(0, tiles, one, 0, unroll=4 if len(strips) < 3 else 2)
 
     def messages(step):
         c.smt[...] = jnp.zeros_like(c.smt)
@@ -619,7 +648,7 @@
             g = c.plan[0, t]
             ch = t - g
             mine = ones_where(iota((GROUP, LO), 0) + g * GROUP == c.tlc[ch])
-            source = c.sc[ch]
+            source = c.sc[ch].astype(F32)
             parts = []
             for j in range(J):
                 row = jnp.broadcast_to(source[j : j + 1, :], (GROUP, LO)).astype(BF16)
@@ -633,11 +662,12 @@
     nodes_here = pl.ds(pl.multiple_of(r * NQ, NQ), NQ)
     groups_here = pl.ds(pl.multiple_of(r * (NQ // GROUP), NQ // GROUP), NQ // GROUP)
     if s.KEEP:
+        near = NEAR + 1
+        first_pass([0], True)
         weight_relay()
+        first_pass(range(1, s.C), False)
         arrive(weight_pair)
-        half = OW // 2
-        first_pass(range(half), True)
-        first_pass(range(half, OW), False)
+        first_pass(range(s.C, OW), False)
     else:
         weight_wait()
     sums = messages(0)
@@ -708,7 +738,7 @@
 
         lax.fori_loop(0, tiles, one, 0, unroll=2)
         rows = pl.ds(ROW_SECOND_BIAS + pl.multiple_of(r * J, J), J)
-        high, low = two(c.ssum[step])
+        high, low = [nn(from_slots, x).astype(BF16) for x in two(c.ssum[step])]
         c.small[rows, :] += nn(high, held) + nn(low, held)
 
     def weights_tile(step, t, second):
@@ -727,7 +757,7 @@
             more = nn(c.w2k[:, rows], outer)
             got = more if got is None else got + more
             if second:
-                c.gacc[rows, :] += nt(outer, take(c.ht, t))
+                c.gacc[rows, :] += nt(outer, hidden_of(t))
         c.hg[:, e] = got
 
     def weights(step, begin, end):
@@ -828,23 +858,23 @@
         return c.gacc[pl.ds(pl.multiple_of(q * per_owner, per_owner), per_owner), :]
 
     if STRIDE == 1:
-        def pieces_in(ref, first):
-            return lambda m: ref.at[pl.ds(pl.multiple_of((first + m) * T, T), T)]
-
-        from_pair, from_chip = pieces_in(c.w2r, 0), pieces_in(c.w2r, s.C)
-        to_pair, to_chip = pieces_in(c.baug, 0), pieces_in(c.baug, s.C)
+        def piece_rows(k):
+            return c.gacc[k * per_owner : (k + 1) * per_owner, :].reshape(T, H, H)
+
+        def pieces_in(ref, k):
+            return ref.at[k * T : (k + 1) * T]
+
         pair = []
         for m in range(s.C):
-            piece = grad_rows(device(m, 1 - core)).astype(BF16).reshape(T, H, H)
-            c.baug[m * T : (m + 1) * T] = piece
+            c.baug[m * T : (m + 1) * T] = piece_rows(s.C + m).astype(BF16)
             x = P_GRAD_PAIR
             cp = push(
-                to_pair(m),
-                from_pair(m),
+                pieces_in(c.baug, m),
+                pieces_in(c.w2r, m),
                 c.ps.at[x, m],
                 c.pr.at[x, m],
                 "blk",
-                device(chip, 1 - core),
+                device(0, 1 - core),
             )
             cp.start()
             pair.append(cp)
@@ -878,23 +908,22 @@
     if STRIDE == 1:
         across = []
         for m in list(range(1, s.C)) + [0]:
-            other = lax.rem(chip + m, s.C)
             if m == 1:
                 arrive(pair)
-            total = grad_rows(device(other, core)).reshape(T, H, H)
-            total = (total + from_pair(other)[...].astype(F32)).astype(BF16)
+            total = piece_rows(m) + c.w2r[m * T : (m + 1) * T].astype(F32)
+            total = total.astype(BF16)
             if m == 0:
-                c.w2r[pl.ds(pl.multiple_of((s.C + chip) * T, T), T)] = total
+                c.w2r[s.C * T : (s.C + 1) * T] = total
                 continue
             c.baug[(s.C + m) * T : (s.C + m + 1) * T] = total
             x = P_GRAD
             cp = push(
-                to_chip(m),
-                from_chip(chip),
+                pieces_in(c.baug, s.C + m),
+                pieces_in(c.w2r, s.C + m),
                 c.ps.at[x, m],
                 c.pr.at[x, m],
                 "blk",
-                device(other, core),
+                device(m, core, True),
             )
             cp.start()
             across.append(cp)
@@ -947,9 +976,17 @@
         arrive(second_in)
 
     when_owner(sum_small)
-    second_relay, second_wait, _, _ = from_owners(
-        P_GRAD_ALL, P_GRAD_ALL_PAIR, lambda q: c.f.at[:, q]
-    )
+    if STRIDE == 1:
+
+        def held_strip(m):
+            strip = c.f.at[:, device(m, core, True)]
+            return strip, strip
+
+        second_relay, second_wait, _, _ = gather_pairs(
+            P_GRAD_ALL, P_GRAD_ALL_PAIR, lambda m: held_strip(0), held_strip
+        )
+    else:
+        second_relay, second_wait, _, _ = from_owners(P_GRAD_ALL, lambda q: c.f.at[:, q])
 
     weights(0, 7, tiles)
 

time: 142 us -> 138 us (0.972)
  Pallas kernels: 140 us -> 137 us
    pallas_call x1, Pallas kernels: 136 us -> 132 us  [body(): pl.pallas_call(functools.partial(whole, s, names), out_shape=[sds((N, H),...]
where the time goes in v4:
time: 138 us
  Pallas kernels  137 us (99%)
  between operations  1.46 us (1%)
    pallas_call x1, Pallas kernels, body(): pl.pallas_call(functools.partial(whole, s, names), out_shape=[sds((N, H),...  132 us
    pallas_call x1, Pallas kernels, body(): pl.pallas_call(functools.partial(finish, s), out_shape=[sds((N, H), F32),...  4.59 us

profile of v4, /device:TPU:0, one launch (start us, length us, event | category | flops | bytes accessed | tf_op | source)
XLA Modules:
  0.0 138.2 jit_solution(2972824425860649936)
XLA Ops:
  1.3 132.1 %edge_network.1 = (f32[512,128]{1,0:T(8,128)}, bf16[512,128]{1,0:T(8,128)(2,1)}, bf16[16,4096]{1,0:T(8,128)(2,1)}, bf16[5,8,128,128]{3,2,1,0:T(8,128)(2,1)}, f32[32,128]{1,0:T(8,128)}) custom-call(f32[512,128]{1,0:T(8,128)} %refs_0_.1, bf16[16,4096]{1,0:T(8,128)(2,1)} %bitcast.15, s32[1,4096]{1,0:T(1,128)} %bitcast.16, s32[1,4096]{1,0:T(1,128)} %bitcast.17, ...), custom_call_target="tpu_custom_call" | custom-call | tf_op jit(solution)/shard_map/edge_network/pallas_call | solution.py:1127
  133.4 4.6 %finish.1 = (f32[512,128]{1,0:T(8,128)}, f32[512,128]{1,0:T(8,128)}, f32[16,4096]{1,0:T(8,128)}, f32[128,4096]{1,0:T(8,128)}, f32[128,384]{1,0:T(8,128)}, /*inde...) custom-call(bf16[5,8,128,128]{3,2,1,0:T(8,128)(2,1)} %get-tuple-elem, ...), custom_call_target="tpu_custom_call" | custom-call | tf_op jit(solution)/shard_map/finish/pallas_call | solution.py:1144

commit v5 on v4

--- a/solution.py
+++ b/solution.py
@@ -513,7 +513,7 @@
                 put(c.sc, t, total.astype(BF16))
             return carry
 
-        lax.fori_loop(0, tiles, one, 0)
+        lax.fori_loop(0, tiles, one, 0, unroll=2)
 
     arrive(states_in)
     gather(0)
@@ -737,6 +737,8 @@
             return carry
 
         lax.fori_loop(0, tiles, one, 0, unroll=2)
+    def second_bias_grads(step):
+        held = c.gfull[step].reshape(N, H)
         rows = pl.ds(ROW_SECOND_BIAS + pl.multiple_of(r * J, J), J)
         high, low = [nn(from_slots, x).astype(BF16) for x in two(c.ssum[step])]
         c.small[rows, :] += nn(high, held) + nn(low, held)
@@ -765,7 +767,7 @@
             weights_tile(step, t, step == STEPS - 1)
             return carry
 
-        lax.fori_loop(begin, end, one, 0)
+        lax.fori_loop(begin, end, one, 0, unroll=2 if step == 0 else 1)
 
     def sources(step, begin, end):
         if begin == 0:
@@ -823,6 +825,7 @@
     node_grads(last)
     sources(last, 0, tiles)
     spread = spread_sources(last)
+    second_bias_grads(last)
     weights(last, 0, 3)
     arrive(spread, reuse=True)
     pieces = share_sources(last)
@@ -893,6 +896,7 @@
         )
 
     node_grads(0)
+    second_bias_grads(0)
 
     c.sgsend[...] = c.small[...].astype(BF16)
 
@@ -965,10 +969,10 @@
 
     when_owner(reduce_grads)
     second_in = line_owner(Z_SECOND, lambda peer: c.gz.at[peer], c.f.at[r, owner])
-    weights(0, 2, 5)
+    weights(0, 2, 6)
     arrive(spread)
     pieces = share_sources(0)
-    weights(0, 5, 7)
+    weights(0, 6, tiles)
 
     def sum_small():
         arrive(small_in)
@@ -988,7 +992,11 @@
     else:
         second_relay, second_wait, _, _ = from_owners(P_GRAD_ALL, lambda q: c.f.at[:, q])
 
-    weights(0, 7, tiles)
+    arrive(pieces)
+    grad = state_grad(0).astype(BF16)
+    c.gradl[...] = grad
+    c.grads[nodes_here, :] = grad
+    grads_in = line(Z_GRADS, lambda peer: c.gradl, c.grads.at[nodes_here, :])
 
     w1 = c.w1[...]
     c.firsts[...] = jnp.zeros_like(c.firsts)
@@ -999,12 +1007,12 @@
         pre = nn(w1ta, mt)
         gate = jax.nn.sigmoid(pre)
         pre_grad = c.hg[:, e] * gate * (1.0 + pre * (1.0 - gate))
-        high, low = two(pre_grad)
-        c.fqs[:, e] = ((nn(w1, high) + nn(w1, low)) * c.gm[:, e].astype(F32)).astype(BF16)
-        c.firsts[...] += nt(mt, high) + nt(mt, low)
+        pre_grad = pre_grad.astype(BF16)
+        c.fqs[:, e] = (nn(w1, pre_grad) * c.gm[:, e].astype(F32)).astype(BF16)
+        c.firsts[...] += nt(mt, pre_grad)
         return carry
 
-    lax.fori_loop(0, tiles, first_layer, 0)
+    lax.fori_loop(0, tiles, first_layer, 0, unroll=2)
     edges_here = pl.ds(pl.multiple_of(r * EQ, EQ), EQ)
     c.fql[r] = c.fqs[:, edges_here]
     feats_in = line(
@@ -1014,12 +1022,6 @@
     )
     c.flz[r] = c.firsts[...]
     firsts_in = line(Z_FIRST, lambda peer: c.firsts, c.flz.at[r])
-
-    arrive(pieces)
-    grad = state_grad(0).astype(BF16)
-    c.gradl[...] = grad
-    c.grads[nodes_here, :] = grad
-    grads_in = line(Z_GRADS, lambda peer: c.gradl, c.grads.at[nodes_here, :])
 
     arrive(feats_in)
     c.ff[:, edges_here] = total_of(c.fql, slice(None), R).astype(BF16)

time: 138 us -> 136 us (0.986)
  Pallas kernels: 137 us -> 134 us
    pallas_call x1, Pallas kernels: 132 us -> 130 us  [body(): pl.pallas_call(functools.partial(whole, s, names), out_shape=[sds((N, H),...]
where the time goes in v5:
time: 136 us
  Pallas kernels  134 us (99%)
  between operations  1.46 us (1%)
    pallas_call x1, Pallas kernels, body(): pl.pallas_call(functools.partial(whole, s, names), out_shape=[sds((N, H),...  130 us
    pallas_call x1, Pallas kernels, body(): pl.pallas_call(functools.partial(finish, s), out_shape=[sds((N, H), F32),...  4.59 us

profile of v5, /device:TPU:0, one launch (start us, length us, event | category | flops | bytes accessed | tf_op | source)
XLA Modules:
  0.0 135.6 jit_solution(16384324623403901263)
XLA Ops:
  1.3 129.5 %edge_network.1 = (f32[512,128]{1,0:T(8,128)}, bf16[512,128]{1,0:T(8,128)(2,1)}, bf16[16,4096]{1,0:T(8,128)(2,1)}, bf16[5,8,128,128]{3,2,1,0:T(8,128)(2,1)}, f32[32,128]{1,0:T(8,128)}) custom-call(f32[512,128]{1,0:T(8,128)} %refs_0_.1, bf16[16,4096]{1,0:T(8,128)(2,1)} %bitcast.15, s32[1,4096]{1,0:T(1,128)} %bitcast.16, s32[1,4096]{1,0:T(1,128)} %bitcast.17, ...), custom_call_target="tpu_custom_call" | custom-call | tf_op jit(solution)/shard_map/edge_network/pallas_call | solution.py:1129
  130.8 4.6 %finish.1 = (f32[512,128]{1,0:T(8,128)}, f32[512,128]{1,0:T(8,128)}, f32[16,4096]{1,0:T(8,128)}, f32[128,4096]{1,0:T(8,128)}, f32[128,384]{1,0:T(8,128)}, /*inde...) custom-call(bf16[5,8,128,128]{3,2,1,0:T(8,128)(2,1)} %get-tuple-elem, ...), custom_call_target="tpu_custom_call" | custom-call | tf_op jit(solution)/shard_map/finish/pallas_call | solution.py:1146

commit v6 on v5

--- a/solution.py
+++ b/solution.py
@@ -164,8 +164,8 @@
         scat=v((s.HI * s.J, LO), F32),
         rps=v((s.B, s.HIB * s.J, LO), BF16),
         rpl=v((STEPS, s.B, s.HIB * s.J, LO), BF16),
-        fzs=v((STEPS, s.R, s.J, s.NQ), F32),
-        fzl=v((STEPS, s.R, s.J, s.NQ), F32),
+        fzs=v((STEPS, s.R, s.J, s.NQ), BF16),
+        fzl=v((STEPS, s.R, s.J, s.NQ), BF16),
         gradq=v((s.NQ, s.H), F32),
         gradl=v((s.NQ, s.H), BF16),
         small=v((SMALL_ROWS, s.H), F32),
@@ -240,7 +240,7 @@
 
     def line(x, src_of, dst):
         copies = []
-        for d in range(1, R):
+        for d in sorted(range(1, R), key=lambda d: abs(d - R / 2)):
             peer = lax.rem(r + d, R)
             cp = push(src_of(peer), dst, c.zs.at[x, d], c.zr.at[x, d], "rep", peer)
             cp.start()
@@ -811,12 +811,12 @@
             total = total + c.rpl[step, q].astype(F32)
         for q in range(R):
             k, lane = (q * NQ) // LO, (q * NQ) % LO
-            c.fzs[step, q] = total[k * J : (k + 1) * J, lane : lane + NQ]
+            c.fzs[step, q] = total[k * J : (k + 1) * J, lane : lane + NQ].astype(BF16)
         c.fzl[step, r] = c.fzs[step, r]
         return line(Z_SOURCE + step, lambda peer: c.fzs.at[step, peer], c.fzl.at[step, r])
 
     def state_grad(step):
-        return c.gradq[...] + c.fzl[step].reshape(H, NQ).T
+        return c.gradq[...] + c.fzl[step].reshape(H, NQ).astype(F32).T
 
     last = STEPS - 1
     copies = deltas(last, c.cot[nodes_here, :])
@@ -969,10 +969,10 @@
 
     when_owner(reduce_grads)
     second_in = line_owner(Z_SECOND, lambda peer: c.gz.at[peer], c.f.at[r, owner])
-    weights(0, 2, 6)
+    weights(0, 2, 4)
     arrive(spread)
     pieces = share_sources(0)
-    weights(0, 6, tiles)
+    weights(0, 4, tiles)
 
     def sum_small():
         arrive(small_in)

time: 136 us -> 134 us (0.985)
  Pallas kernels: 134 us -> 132 us
    pallas_call x1, Pallas kernels: 130 us -> 128 us  [body(): pl.pallas_call(functools.partial(whole, s, names), out_shape=[sds((N, H),...]
where the time goes in v6:
time: 134 us
  Pallas kernels  132 us (99%)
  between operations  1.46 us (1%)
    pallas_call x1, Pallas kernels, body(): pl.pallas_call(functools.partial(whole, s, names), out_shape=[sds((N, H),...  128 us
    pallas_call x1, Pallas kernels, body(): pl.pallas_call(functools.partial(finish, s), out_shape=[sds((N, H), F32),...  4.59 us

profile of v6, /device:TPU:0, one launch (start us, length us, event | category | flops | bytes accessed | tf_op | source)
XLA Modules:
  0.0 133.8 jit_solution(9144308136334985069)
XLA Ops:
  1.3 127.7 %edge_network.1 = (f32[512,128]{1,0:T(8,128)}, bf16[512,128]{1,0:T(8,128)(2,1)}, bf16[16,4096]{1,0:T(8,128)(2,1)}, bf16[5,8,128,128]{3,2,1,0:T(8,128)(2,1)}, f32[32,128]{1,0:T(8,128)}) custom-call(f32[512,128]{1,0:T(8,128)} %refs_0_.1, bf16[16,4096]{1,0:T(8,128)(2,1)} %bitcast.15, s32[1,4096]{1,0:T(1,128)} %bitcast.16, s32[1,4096]{1,0:T(1,128)} %bitcast.17, ...), custom_call_target="tpu_custom_call" | custom-call | tf_op jit(solution)/shard_map/edge_network/pallas_call | solution.py:1129
  129.0 4.6 %finish.1 = (f32[512,128]{1,0:T(8,128)}, f32[512,128]{1,0:T(8,128)}, f32[16,4096]{1,0:T(8,128)}, f32[128,4096]{1,0:T(8,128)}, f32[128,384]{1,0:T(8,128)}, /*inde...) custom-call(bf16[5,8,128,128]{3,2,1,0:T(8,128)(2,1)} %get-tuple-elem, ...), custom_call_target="tpu_custom_call" | custom-call | tf_op jit(solution)/shard_map/finish/pallas_call | solution.py:1146
